TPU v7x, 512 devices: a whole 4x4x16 slice. The times are simulated.
512 devices in a mesh: grp: 4 (over x_lo, core), gx: 8 (over y, x_hi), gy: 16 (over z).
Axes of the slice: x: 4 (x_hi: 2, x_lo: 2; x = x_hi * 2 + x_lo), y: 4, z: 16, core: 2. Of those that a mesh axis runs over, the one named last changes fastest.
Arguments:
- pressure: float32 [24, 512, 4096], P(None, ('grp', 'gy'), 'gx'), may hold values from -2 to 0.2
- soil_class: int32 [24, 512, 4096], P(None, ('grp', 'gy'), 'gx'), may hold values from 0 to 11
- capacity_range: float32 [12], replicated, may hold values from 0.25 to 0.45
- inverse_entry: float32 [12], replicated, may hold values from 0.3 to 3
- shape_index: float32 [12], replicated, may hold values from 1.3 to 2.5
- conductivity: float32 [12], replicated, may hold values from 0.05 to 1
- depth: float32 [512, 4096], P('grp', ('gx', 'gy')), may hold values from 0 to 2
- elevation: float32 [512, 4096], P('grp', ('gx', 'gy')), may hold values from -4 to 4
- roughness: float32 [512, 4096], P('grp', ('gx', 'gy')), may hold values from 2 to 8
- rain: float32 [512, 4096], P('grp', ('gx', 'gy')), may hold values from 0.1 to 1
- land_mask: int32 [512, 4096], P('grp', ('gx', 'gy')), may hold values 0 or 1
- channel_mask: int32 [512, 4096], P('grp', ('gx', 'gy')), may hold values 0 or 1
Outputs:
- head: float32 [24, 512, 4096], P(None, ('grp', 'gy'), 'gx')
- water: float32 [512, 4096], P('grp', ('gx', 'gy'))
All inputs are finite; a program needn't handle non-finite values. No bound on the sum of `land_mask` or of `channel_mask` on one device may be relied on, other than what follows from the above.
Results may differ from a plain program's by a relative error of at most 0.0003.
Values sent between devices are 32-bit elements; how exact they have to be, the bound alone decides.
A program may use at most 64 MiB of HBM per device.

v0:
```python
import jax
import jax.numpy as jnp
from jax import lax
from jax.sharding import PartitionSpec as P

SWEEPS = 2
PASSES = 3


STORAGE = 0.01
LATERAL = 4.0
VERTICAL = 4.0
GRAVITY_STEP = 0.5
SUCTION_FLOOR = 0.01
SLOPE_FLOOR = 0.1
SURFACE_STEP = 0.3
LEAKANCE = 0.5
SOURCE_GAIN = 1.0


def with_halo(shard, sides, width):
    for axis, dim in sides:
        size, length = (lax.axis_size(axis), shard.shape[dim])
        up = [(i, (i + 1) % size) for i in range(size - 1)]
        down = [(j, i) for i, j in up]
        last = lax.slice_in_dim(shard, length - width, length, axis=dim)
        leading = lax.slice_in_dim(shard, 0, width, axis=dim)
        before = lax.ppermute(last, axis, up)
        after = lax.ppermute(leading, axis, down)
        shard = jnp.concatenate([before, shard, after], axis=dim)
    return shard


def padded_2(shard, sides, width):
    edges = {}
    for axis, dim in sides:
        size, length = (lax.axis_size(axis), shard.shape[dim])
        up = [(i, (i + 1) % size) for i in range(size - 1)]
        last = lax.slice_in_dim(shard, length - width, length, axis=dim)
        leading = lax.slice_in_dim(shard, 0, width, axis=dim)
        edges[dim] = (
            lax.ppermute(last, axis, up),
            lax.ppermute(leading, axis, [(b, a) for a, b in up]),
        )
    done = []
    for _, dim in sides:
        low, high = edges[dim]
        around = [(width, width) if d in done else (0, 0) for d in range(shard.ndim)]
        shard = jnp.concatenate([jnp.pad(low, around), shard, jnp.pad(high, around)], axis=dim)
        done.append(dim)
    return shard


def lookup(soil_class, tables):
    results = []
    for table in tables:
        filled = jnp.zeros(soil_class.shape, table.dtype)
        for kind_number in range(table.shape[0]):
            filled = jnp.where(soil_class == kind_number, table[kind_number], filled)
        results.append(filled)
    return results


def closures(pressure, capacity_range, inverse_entry, pore_index, conductivity):
    exponent = 1.0 / (1.0 - pore_index)
    scaled = jnp.maximum(-inverse_entry * pressure, SUCTION_FLOOR)
    log_scaled = jnp.log(scaled)
    log_sum = jnp.log1p(jnp.exp(exponent * log_scaled))
    saturation = jnp.exp(-pore_index * log_sum)
    content = capacity_range * saturation
    capacity = STORAGE + capacity_range * pore_index * exponent * inverse_entry * jnp.exp(
        (exponent - 1.0) * log_scaled - (pore_index + 1.0) * log_sum
    )
    conduct = (
        conductivity
        * jnp.sqrt(saturation)
        * jnp.square(1.0 - jnp.exp(pore_index * (exponent * log_scaled - log_sum)))
    )
    return (content, capacity, conduct)


def update_cells(padded, conduct_pad, capacity, content_gap, source):
    layers = padded.shape[0] - 2
    rows = padded.shape[1] - 2
    cols = padded.shape[2] - 2
    center = padded[1:-1, 1:-1, 1:-1]
    own_conduct = conduct_pad[1:-1, 1:-1, 1:-1]
    numerator = capacity * center - content_gap
    denominator = capacity
    neighbours = (
        (1, 0, 1, LATERAL, 0.0),
        (1, 2, 1, LATERAL, 0.0),
        (1, 1, 0, LATERAL, 0.0),
        (1, 1, 2, LATERAL, 0.0),
        (0, 1, 1, VERTICAL, GRAVITY_STEP),
        (2, 1, 1, VERTICAL, -GRAVITY_STEP),
    )
    for first, second, third, weight, offset in neighbours:
        beside = padded[first : first + layers, second : second + rows, third : third + cols]
        beside_conduct = conduct_pad[
            first : first + layers, second : second + rows, third : third + cols
        ]
        face_weight = weight * jnp.sqrt(own_conduct * beside_conduct)
        numerator = numerator + face_weight * (beside + offset)
        denominator = denominator + face_weight
    gained = jnp.concatenate(
        [(SOURCE_GAIN * source)[None], jnp.zeros((layers - 1, rows, cols), source.dtype)], axis=0
    )
    numerator = numerator + gained
    return numerator / denominator


def face_flux(upper_level, lower_level, upper_depth, lower_depth, upper_convey, lower_convey):
    slope = upper_level - lower_level
    upwind = jnp.where(slope >= 0, upper_depth, lower_depth)
    carried = upwind * jnp.cbrt(upwind * upwind)
    return (
        jnp.sqrt(upper_convey * lower_convey)
        * carried
        * slope
        / jnp.sqrt(jnp.maximum(jnp.abs(slope), SLOPE_FLOOR))
    )


def overland(depth_pad, level_pad, convey_pad, leak, top, rain):
    current = depth_pad[1:-1, 1:-1]
    surface = level_pad + depth_pad
    across = face_flux(
        surface[:-1, 1:-1],
        surface[1:, 1:-1],
        depth_pad[:-1, 1:-1],
        depth_pad[1:, 1:-1],
        convey_pad[:-1, 1:-1],
        convey_pad[1:, 1:-1],
    )
    along = face_flux(
        surface[1:-1, :-1],
        surface[1:-1, 1:],
        depth_pad[1:-1, :-1],
        depth_pad[1:-1, 1:],
        convey_pad[1:-1, :-1],
        convey_pad[1:-1, 1:],
    )
    outflow = across[1:] - across[:-1] + (along[:, 1:] - along[:, :-1])
    rate = leak * (current - top)
    return (jnp.maximum(current + SURFACE_STEP * (rain - rate - outflow), 0.0), rate)


def trim_edges(field, margin):
    rows = field.shape[-2]
    cols = field.shape[-1]
    return field[..., margin : rows - margin, margin : cols - margin]


def pad_layers(field):
    return jnp.pad(field, ((1, 1), (0, 0), (0, 0)))


def local(
    pressure,
    soil_class,
    capacity_range,
    inverse_entry,
    shape_index,
    conductivity,
    depth,
    elevation,
    roughness,
    rain,
    land_mask,
    channel_mask,
):
    pore_table = 1.0 - 1.0 / shape_index
    tables = (capacity_range, inverse_entry, pore_table, conductivity)
    range_cells, entry_cells, pore_cells, conduct_cells = lookup(soil_class, tables)
    content0, capacity, conduct = closures(
        pressure, range_cells, entry_cells, pore_cells, conduct_cells
    )
    top_conduct = conduct[0]
    top, top_surface = (
        lax.all_to_all(pressure[0], "gy", split_axis=1, concat_axis=0, tiled=True),
        lax.all_to_all(top_conduct, "gy", split_axis=1, concat_axis=0, tiled=True),
    )
    leak = LEAKANCE * land_mask.astype(jnp.float32) * top_surface
    convey = (1.0 + channel_mask.astype(jnp.float32)) / roughness
    exchange = jnp.zeros_like(depth)
    surface_pad = with_halo(
        jnp.stack([depth, elevation, convey, leak, top, rain]),
        (("grp", 1), (("gx", "gy"), 2)),
        PASSES,
    )
    water = surface_pad[0]
    for pass_number in range(PASSES):
        water, rate = overland(
            water,
            trim_edges(surface_pad[1], pass_number),
            trim_edges(surface_pad[2], pass_number),
            trim_edges(surface_pad[3], pass_number + 1),
            trim_edges(surface_pad[4], pass_number + 1),
            trim_edges(surface_pad[5], pass_number + 1),
        )
        exchange = exchange + SURFACE_STEP * trim_edges(rate, PASSES - pass_number - 1)
    source = lax.all_to_all(exchange, "gy", split_axis=0, concat_axis=1, tiled=True)
    head = pressure
    content = content0
    for sweep_number in range(SWEEPS):
        soil_rim = padded_2(jnp.stack([head, conduct]), ((("grp", "gy"), 2), ("gx", 3)), 1)
        head = update_cells(
            pad_layers(soil_rim[0]), pad_layers(soil_rim[1]), capacity, content - content0, source
        )
        if sweep_number + 1 < SWEEPS:
            content, capacity, conduct = closures(
                head, range_cells, entry_cells, pore_cells, conduct_cells
            )
    return (head, water)


def solution(mesh):
    return jax.shard_map(
        local,
        mesh=mesh,
        in_specs=(
            P(None, ("grp", "gy"), "gx"),
            P(None, ("grp", "gy"), "gx"),
            P(),
            P(),
            P(),
            P(),
            P("grp", ("gx", "gy")),
            P("grp", ("gx", "gy")),
            P("grp", ("gx", "gy")),
            P("grp", ("gx", "gy")),
            P("grp", ("gx", "gy")),
            P("grp", ("gx", "gy")),
        ),
        out_specs=(P(None, ("grp", "gy"), "gx"), P("grp", ("gx", "gy"))),
        check_vma=False,
    )
```

profile of v0, /device:TPU:14, one launch (start us, length us, event | category | flops | bytes accessed | tf_op | source)
XLA Modules:
  0.0 175.4 jit_solution(9895677468725796181)
XLA Ops:
  0.6 0.7 slice.601
  2.2 15.2 %all-to-all-start.1 = ((f32[16,1,256]{2,1,0:T(1,128)}), f32[16,1,256]{2,1,0:T(1,128)S(1)}, u32[]{:S(2)}, u32[]{:S(2)}) async-start(f32[16,1,256]{2,1,0:T(1,128)} %reshape.19), calls=%async_computation.1 | async-start | bytes 32768 | tf_op jit(solution)/shard_map/all_to_all | solution.py:181
  18.7 1.8 %fusion.119 = (f32[1]{0:T(128)}, f32[1]{0:T(128)}, f32[1]{0:T(128)}, f32[1]{0:T(128)}, f32[1]{0:T(128)}, /*index=5*/f32[1]{0:T(128)}, f32[1]{0:T(128)}, f32[1]{0...) fusion(f32[12]{0:T(128)} %param.15), kind=kLoop, calls=%fused_computation.241 | loop fusion | bytes 96 | tf_op jit(solution)/shard_map/slice | solution.py:59
  20.5 1.8 %fusion.118 = (f32[1]{0:T(128)}, f32[1]{0:T(128)}, f32[1]{0:T(128)}, f32[1]{0:T(128)}, f32[1]{0:T(128)}, /*index=5*/f32[1]{0:T(128)}, f32[1]{0:T(128)}, f32[1]{0...) fusion(f32[12]{0:T(128)} %param.17), kind=kLoop, calls=%fused_computation.240 | loop fusion | bytes 96 | tf_op jit(solution)/shard_map/slice | solution.py:59
  22.4 26.3 %multiply_multiply_fusion = (f32[24,8,512]{2,1,0:T(8,128)S(1)}, f32[24,8,512]{2,1,0:T(8,128)S(1)}, f32[24,8,512]{2,1,0:T(8,128)}, f32[24,8,512]{2,1,0:T(8,128)},...) fusion(f32[24,8,512]{2,1,0:T(8,128)} %param.12, ...), kind=kLoop, calls=%fused_computation.109 | loop fusion | flops 6094848 | bytes 3539088 | tf_op jit(solution)/shard_map/mul | solution.py:75
  48.7 0.8 fusion.61
  49.4 3.8 %collective-permute-start.1 = (f32[2,24,1,512]{3,2,1,0:T(1,128)}, f32[2,24,1,512]{3,2,1,0:T(1,128)}, u32[]{:S(2)}, u32[]{:S(2)}) collective-permute-start(f32[2,24,1,512]{3,2,1,0:T(1,128)} %get-tuple-element.41), channel_id=1, source_target_pairs={{0,1},{1,2},{2,3},{3,4},{4,5},{5,6},{6,7},{7,8},{8,9},{9,10},{10,1... | collective-permute-start | bytes 294920 | tf_op jit(solution)/shard_map/ppermute | solution.py:42
  53.3 3.8 %collective-permute-start.2 = (f32[2,24,1,512]{3,2,1,0:T(1,128)}, f32[2,24,1,512]{3,2,1,0:T(1,128)}, u32[]{:S(2)}, u32[]{:S(2)}) collective-permute-start(f32[2,24,1,512]{3,2,1,0:T(1,128)} %get-tuple-element.42), channel_id=1, source_target_pairs={{1,0},{2,1},{3,2},{4,3},{5,4},{6,5},{7,6},{8,7},{9,8},{10,9},{11,1... | collective-permute-start | bytes 294920 | tf_op jit(solution)/shard_map/ppermute | solution.py:43
  58.1 11.5 %all-to-all-start = ((f32[16,1,256]{2,1,0:T(1,128)}), f32[16,1,256]{2,1,0:T(1,128)S(1)}, u32[]{:S(2)}, u32[]{:S(2)}) async-start(f32[16,1,256]{2,1,0:T(1,128)} %reshape.17), calls=%async_computation | async-start | bytes 32768 | tf_op jit(solution)/shard_map/all_to_all | solution.py:182
  71.1 11.1 %all-to-all-done = f32[16,1,256]{2,1,0:T(1,128)S(1)} async-done(((f32[16,1,256]{2,1,0:T(1,128)}), f32[16,1,256]{2,1,0:T(1,128)S(1)}, u32[]{:S(2)}, u32[]{:S(2)}) %all-to-all-start) | async-done | bytes 16416 | tf_op jit(solution)/shard_map/all_to_all | solution.py:182
  83.2 1.9 %collective-permute-start.4 = (f32[6,3,32]{1,2,0:T(8,128)S(1)}, f32[6,3,32]{1,2,0:T(8,128)S(1)}, u32[]{:S(2)}, u32[]{:S(2)}) collective-permute-start(f32[6,3,32]{1,2,0:T(8,128)S(1)} %get-tuple-element.55), channel_id=1, source_target_pairs={{0,128},{128,256},{256,384},{1,129},{129,257},{257,385},{2,130},{1... | collective-permute-start | bytes 6920 | tf_op jit(solution)/shard_map/ppermute | solution.py:28
  85.1 3.6 %collective-permute-start.5 = (f32[6,3,32]{1,2,0:T(8,128)S(1)}, f32[6,3,32]{1,2,0:T(8,128)S(1)}, u32[]{:S(2)}, u32[]{:S(2)}) collective-permute-start(f32[6,3,32]{1,2,0:T(8,128)S(1)} %get-tuple-element.56), channel_id=1, source_target_pairs={{128,0},{256,128},{384,256},{129,1},{257,129},{385,257},{130,2},{2... | collective-permute-start | bytes 6920 | tf_op jit(solution)/shard_map/ppermute | solution.py:29
  88.8 0.8 fusion.57
  89.6 4.3 %collective-permute-start = (f32[2,24,8,1]{3,2,1,0:T(8,128)}, f32[2,24,8,1]{3,2,1,0:T(8,128)}, u32[]{:S(2)}, u32[]{:S(2)}) collective-permute-start(f32[2,24,8,1]{3,2,1,0:T(8,128)} %get-tuple-element.43), channel_id=1, source_target_pairs={{0,16},{16,32},{32,48},{48,64},{64,80},{80,96},{96,112},{1,17},{17... | collective-permute-start | bytes 4616 | tf_op jit(solution)/shard_map/ppermute | solution.py:42
  94.5 3.2 %collective-permute-start.7 = (f32[6,134,3]{2,1,0:T(8,128)S(1)}, f32[6,134,3]{2,1,0:T(8,128)S(1)}, u32[]{:S(2)}, u32[]{:S(2)}) collective-permute-start(f32[6,134,3]{2,1,0:T(8,128)S(1)} %copy.42), channel_id=1, source_target_pairs={{1,0},{2,1},{3,2},{4,3},{5,4},{6,5},{7,6},{8,7},{9,8},{10,9},{11,1... | collective-permute-start | bytes 28952 | tf_op jit(solution)/shard_map/ppermute | solution.py:29
  97.7 2.6 %collective-permute-start.6 = (f32[6,134,3]{2,1,0:T(8,128)S(1)}, f32[6,134,3]{2,1,0:T(8,128)S(1)}, u32[]{:S(2)}, u32[]{:S(2)}) collective-permute-start(f32[6,134,3]{2,1,0:T(8,128)S(1)} %copy.41), channel_id=1, source_target_pairs={{0,1},{1,2},{2,3},{3,4},{4,5},{5,6},{6,7},{7,8},{8,9},{9,10},{10,1... | collective-permute-start | bytes 28952 | tf_op jit(solution)/shard_map/ppermute | solution.py:28
  101.3 5.2 %collective-permute-done.7 = f32[6,134,3]{2,1,0:T(8,128)S(1)} collective-permute-done((f32[6,134,3]{2,1,0:T(8,128)S(1)}, f32[6,134,3]{2,1,0:T(8,128)S(1)}, u32[]{:S(2)}, u32[]{:S(2)}) %collective-permute-start.7) | collective-permute-done | bytes 9680 | tf_op jit(solution)/shard_map/ppermute | solution.py:29
  106.5 3.0 %collective-permute-start.3 = (f32[2,24,8,1]{3,2,1,0:T(8,128)}, f32[2,24,8,1]{3,2,1,0:T(8,128)S(1)}, u32[]{:S(2)}, u32[]{:S(2)}) collective-permute-start(f32[2,24,8,1]{3,2,1,0:T(8,128)} %get-tuple-element.44), channel_id=1, source_target_pairs={{16,0},{32,16},{48,32},{64,48},{80,64},{96,80},{112,96},{17,1},{33... | collective-permute-start | bytes 4616 | tf_op jit(solution)/shard_map/ppermute | solution.py:43
  109.5 3.6 %collective-permute-done.6 = f32[6,134,3]{2,1,0:T(8,128)S(1)} collective-permute-done((f32[6,134,3]{2,1,0:T(8,128)S(1)}, f32[6,134,3]{2,1,0:T(8,128)S(1)}, u32[]{:S(2)}, u32[]{:S(2)}) %collective-permute-start.6) | collective-permute-done | bytes 9680 | tf_op jit(solution)/shard_map/ppermute | solution.py:28
  115.0 0.8 fusion.98
  116.5 3.7 %all-to-all-start.2 = ((f32[16,1,256]{2,1,0:T(1,128)}), f32[16,1,256]{2,1,0:T(1,128)S(1)}, u32[]{:S(2)}, u32[]{:S(2)}) async-start(f32[16,1,256]{2,1,0:T(1,128)} %reshape.21), calls=%async_computation.2 | async-start | bytes 32768 | tf_op jit(solution)/shard_map/all_to_all | solution.py:203
  120.2 2.4 %select_maximum_fusion.2 = f32[2,24,10,514]{3,2,1,0:T(8,128)S(1)} fusion(f32[2,24,8,1]{3,2,1,0:T(8,128)S(1)} %collective-permute-done.3, f32[2,24,8,1]{3,2,1,0:T(8,128)} %collective-permute-done, f32[2,24,1,512]{3,2,1,0:T(1,128)} %collective-permute-done.2, f32[1,24,8,512]{3,2,1,0:T(8,128)S(1)} %bitcast.118, f32[1,24,8,512]{3,2,1,0:T(8,128)S(1)} %bitcast.112, ...), kind=kLoop, calls=%fused_computation.2 | loop fusion | flops 2220480 | bytes 1972992 | tf_op jit(solution)/shard_map/concatenate | solution.py:49
  122.8 9.6 %all-to-all-done.2 = f32[16,1,256]{2,1,0:T(1,128)S(1)} async-done(((f32[16,1,256]{2,1,0:T(1,128)}), f32[16,1,256]{2,1,0:T(1,128)S(1)}, u32[]{:S(2)}, u32[]{:S(2)}) %all-to-all-start.2) | async-done | bytes 16416 | tf_op jit(solution)/shard_map/all_to_all | solution.py:203
  133.2 12.6 %multiply_bitcast_fusion = (f32[1,24,8,512]{3,2,1,0:T(8,128)S(1)}, f32[24,8,512]{2,1,0:T(8,128)S(1)}, f32[24,8,512]{2,1,0:T(8,128)}) fusion(f32[24,8,512]{2,1,0:T(8,128)} %get-tuple-element.20, f32[24,8,512]{2,1,0:T(8,128)} %get-tuple-element.19, f32[24,8,512]{2,1,0:T(8,128)S(1)} %get-tuple-element.18, f32[1,8,512]{2,1,0:T(8,128)S(1)} %broadcast_in_dim.197, ...), kind=kLoop, calls=%fused_computation.103 | loop fusion | flops 7667712 | bytes 9846832 | tf_op jit(solution)/shard_map/stack | solution.py:207
  145.9 2.5 %collective-permute-start.9 = (f32[2,24,1,512]{3,2,1,0:T(1,128)S(1)}, f32[2,24,1,512]{3,2,1,0:T(1,128)S(1)}, u32[]{:S(2)}, u32[]{:S(2)}) collective-permute-start(f32[2,24,1,512]{3,2,1,0:T(1,128)S(1)} %get-tuple-element.37), channel_id=1, source_target_pairs={{0,1},{1,2},{2,3},{3,4},{4,5},{5,6},{6,7},{7,8},{8,9},{9,10},{10,1... | collective-permute-start | bytes 294920 | tf_op jit(solution)/shard_map/ppermute | solution.py:42
  148.4 5.2 %collective-permute-start.10 = (f32[2,24,1,512]{3,2,1,0:T(1,128)S(1)}, f32[2,24,1,512]{3,2,1,0:T(1,128)S(1)}, u32[]{:S(2)}, u32[]{:S(2)}) collective-permute-start(f32[2,24,1,512]{3,2,1,0:T(1,128)S(1)} %get-tuple-element.38), channel_id=1, source_target_pairs={{1,0},{2,1},{3,2},{4,3},{5,4},{6,5},{7,6},{8,7},{9,8},{10,9},{11,1... | collective-permute-start | bytes 294920 | tf_op jit(solution)/shard_map/ppermute | solution.py:43
  153.8 6.1 %collective-permute-start.8 = (f32[2,24,8,1]{3,2,1,0:T(8,128)S(1)}, f32[2,24,8,1]{3,2,1,0:T(8,128)S(1)}, u32[]{:S(2)}, u32[]{:S(2)}) collective-permute-start(f32[2,24,8,1]{3,2,1,0:T(8,128)S(1)} %get-tuple-element.39), channel_id=1, source_target_pairs={{0,16},{16,32},{32,48},{48,64},{64,80},{80,96},{96,112},{1,17},{17... | collective-permute-start | bytes 4616 | tf_op jit(solution)/shard_map/ppermute | solution.py:42
  159.9 1.9 %collective-permute-start.11 = (f32[2,24,8,1]{3,2,1,0:T(8,128)S(1)}, f32[2,24,8,1]{3,2,1,0:T(8,128)S(1)}, u32[]{:S(2)}, u32[]{:S(2)}) collective-permute-start(f32[2,24,8,1]{3,2,1,0:T(8,128)S(1)} %get-tuple-element.40), channel_id=1, source_target_pairs={{16,0},{32,16},{48,32},{64,48},{80,64},{96,80},{112,96},{17,1},{33... | collective-permute-start | bytes 4616 | tf_op jit(solution)/shard_map/ppermute | solution.py:43
  163.2 6.6 %collective-permute-done.11 = f32[2,24,8,1]{3,2,1,0:T(8,128)S(1)} collective-permute-done((f32[2,24,8,1]{3,2,1,0:T(8,128)S(1)}, f32[2,24,8,1]{3,2,1,0:T(8,128)S(1)}, u32[]{:S(2)}, u32[]{:S(2)}) %collective-permute-start.11) | collective-permute-done | bytes 1568 | tf_op jit(solution)/shard_map/ppermute | solution.py:43
  169.9 1.4 select_maximum_fusion
  171.4 0.8 copy-done.1
  172.4 3.1 %fusion.1 = f32[24,8,512]{2,1,0:T(8,128)} fusion(f32[1,8,512]{2,1,0:T(8,128)S(1)} %broadcast_in_dim.197, f32[24,10,514]{2,1,0:T(8,128)S(1)} %get-tuple-element.34, f32[24,10,514]{2,1,0:T(8,128)S(1)} %get-tuple-element.33, f32[24,8,512]{2,1,0:T(8,128)S(1)} %copy-done.2, f32[24,8,512]{2,1,0:T(8,128)S(1)} %copy-done.1, f32[24,8,512]{2,1,0:T(8,128)S(1)} %get-tuple-element.18, ...), kind=kLoop, calls=%fused_computation.34 | loop fusion | flops 5996544 | bytes 8273920 | tf_op jit(solution)/shard_map/div | solution.py:110
  (84 shorter events, 12.3 us)
Async XLA Ops:
  1.4 47.2 %copy-start = (f32[24,8,512]{2,1,0:T(8,128)S(1)}, f32[24,8,512]{2,1,0:T(8,128)}, u32[]{:S(2)}) copy-start(f32[24,8,512]{2,1,0:T(8,128)} %param.12) | copy-start | bytes 1179652
  2.2 56.0 %all-to-all-start.1 = ((f32[16,1,256]{2,1,0:T(1,128)}), f32[16,1,256]{2,1,0:T(1,128)S(1)}, u32[]{:S(2)}, u32[]{:S(2)}) async-start(f32[16,1,256]{2,1,0:T(1,128)} %reshape.19), calls=%async_computation.1 | async-start | bytes 32768 | tf_op jit(solution)/shard_map/all_to_all | solution.py:181
  22.3 34.8 %copy-start.8 = (f32[128,32]{0,1:T(8,128)S(1)}, f32[128,32]{0,1:T(8,128)}, u32[]{:S(2)}) copy-start(f32[128,32]{0,1:T(8,128)} %param.18) | copy-start | bytes 49156
  22.3 34.8 %copy-start.9 = (f32[128,32]{0,1:T(8,128)S(1)}, f32[128,32]{0,1:T(8,128)}, u32[]{:S(2)}) copy-start(f32[128,32]{0,1:T(8,128)} %param.19) | copy-start | bytes 49156
  22.3 34.8 %copy-start.5 = (f32[128,32]{0,1:T(8,128)S(1)}, f32[128,32]{0,1:T(8,128)}, u32[]{:S(2)}) copy-start(f32[128,32]{0,1:T(8,128)} %param.20) | copy-start | bytes 49156
  22.3 34.8 %copy-start.6 = (s32[128,32]{0,1:T(8,128)S(1)}, s32[128,32]{0,1:T(8,128)}, u32[]{:S(2)}) copy-start(s32[128,32]{0,1:T(8,128)} %param.23) | copy-start | bytes 49156
  22.4 34.9 %copy-start.7 = (s32[128,32]{0,1:T(8,128)S(1)}, s32[128,32]{0,1:T(8,128)}, u32[]{:S(2)}) copy-start(s32[128,32]{0,1:T(8,128)} %param.22) | copy-start | bytes 49156
  48.6 34.4 %copy-start.10 = (f32[128,32]{0,1:T(8,128)S(1)}, f32[128,32]{0,1:T(8,128)}, u32[]{:S(2)}) copy-start(f32[128,32]{0,1:T(8,128)} %param.21) | copy-start | bytes 49156
  49.4 70.8 %collective-permute-start.1 = (f32[2,24,1,512]{3,2,1,0:T(1,128)}, f32[2,24,1,512]{3,2,1,0:T(1,128)}, u32[]{:S(2)}, u32[]{:S(2)}) collective-permute-start(f32[2,24,1,512]{3,2,1,0:T(1,128)} %get-tuple-element.41), channel_id=1, source_target_pairs={{0,1},{1,2},{2,3},{3,4},{4,5},{5,6},{6,7},{7,8},{8,9},{9,10},{10,1... | collective-permute-start | bytes 294920 | tf_op jit(solution)/shard_map/ppermute | solution.py:42
  53.3 67.0 %collective-permute-start.2 = (f32[2,24,1,512]{3,2,1,0:T(1,128)}, f32[2,24,1,512]{3,2,1,0:T(1,128)}, u32[]{:S(2)}, u32[]{:S(2)}) collective-permute-start(f32[2,24,1,512]{3,2,1,0:T(1,128)} %get-tuple-element.42), channel_id=1, source_target_pairs={{1,0},{2,1},{3,2},{4,3},{5,4},{6,5},{7,6},{8,7},{9,8},{10,9},{11,1... | collective-permute-start | bytes 294920 | tf_op jit(solution)/shard_map/ppermute | solution.py:43
  58.1 42.2 %copy-start.4 = (f32[12]{0:T(128)S(1)}, f32[12]{0:T(128)}, u32[]{:S(2)}) copy-start(f32[12]{0:T(128)} %param.14) | copy-start | bytes 148
  58.1 24.1 %all-to-all-start = ((f32[16,1,256]{2,1,0:T(1,128)}), f32[16,1,256]{2,1,0:T(1,128)S(1)}, u32[]{:S(2)}, u32[]{:S(2)}) async-start(f32[16,1,256]{2,1,0:T(1,128)} %reshape.17), calls=%async_computation | async-start | bytes 32768 | tf_op jit(solution)/shard_map/all_to_all | solution.py:182
  83.2 10.7 %collective-permute-start.4 = (f32[6,3,32]{1,2,0:T(8,128)S(1)}, f32[6,3,32]{1,2,0:T(8,128)S(1)}, u32[]{:S(2)}, u32[]{:S(2)}) collective-permute-start(f32[6,3,32]{1,2,0:T(8,128)S(1)} %get-tuple-element.55), channel_id=1, source_target_pairs={{0,128},{128,256},{256,384},{1,129},{129,257},{257,385},{2,130},{1... | collective-permute-start | bytes 6920 | tf_op jit(solution)/shard_map/ppermute | solution.py:28
  85.1 8.8 %collective-permute-start.5 = (f32[6,3,32]{1,2,0:T(8,128)S(1)}, f32[6,3,32]{1,2,0:T(8,128)S(1)}, u32[]{:S(2)}, u32[]{:S(2)}) collective-permute-start(f32[6,3,32]{1,2,0:T(8,128)S(1)} %get-tuple-element.56), channel_id=1, source_target_pairs={{128,0},{256,128},{384,256},{129,1},{257,129},{385,257},{130,2},{2... | collective-permute-start | bytes 6920 | tf_op jit(solution)/shard_map/ppermute | solution.py:29
  89.6 30.6 %collective-permute-start = (f32[2,24,8,1]{3,2,1,0:T(8,128)}, f32[2,24,8,1]{3,2,1,0:T(8,128)}, u32[]{:S(2)}, u32[]{:S(2)}) collective-permute-start(f32[2,24,8,1]{3,2,1,0:T(8,128)} %get-tuple-element.43), channel_id=1, source_target_pairs={{0,16},{16,32},{32,48},{48,64},{64,80},{80,96},{96,112},{1,17},{17... | collective-permute-start | bytes 4616 | tf_op jit(solution)/shard_map/ppermute | solution.py:42
  94.5 11.9 %collective-permute-start.7 = (f32[6,134,3]{2,1,0:T(8,128)S(1)}, f32[6,134,3]{2,1,0:T(8,128)S(1)}, u32[]{:S(2)}, u32[]{:S(2)}) collective-permute-start(f32[6,134,3]{2,1,0:T(8,128)S(1)} %copy.42), channel_id=1, source_target_pairs={{1,0},{2,1},{3,2},{4,3},{5,4},{6,5},{7,6},{8,7},{9,8},{10,9},{11,1... | collective-permute-start | bytes 28952 | tf_op jit(solution)/shard_map/ppermute | solution.py:29
  97.7 15.4 %collective-permute-start.6 = (f32[6,134,3]{2,1,0:T(8,128)S(1)}, f32[6,134,3]{2,1,0:T(8,128)S(1)}, u32[]{:S(2)}, u32[]{:S(2)}) collective-permute-start(f32[6,134,3]{2,1,0:T(8,128)S(1)} %copy.41), channel_id=1, source_target_pairs={{0,1},{1,2},{2,3},{3,4},{4,5},{5,6},{6,7},{7,8},{8,9},{9,10},{10,1... | collective-permute-start | bytes 28952 | tf_op jit(solution)/shard_map/ppermute | solution.py:28
  106.5 13.7 %collective-permute-start.3 = (f32[2,24,8,1]{3,2,1,0:T(8,128)}, f32[2,24,8,1]{3,2,1,0:T(8,128)S(1)}, u32[]{:S(2)}, u32[]{:S(2)}) collective-permute-start(f32[2,24,8,1]{3,2,1,0:T(8,128)} %get-tuple-element.44), channel_id=1, source_target_pairs={{16,0},{32,16},{48,32},{64,48},{80,64},{96,80},{112,96},{17,1},{33... | collective-permute-start | bytes 4616 | tf_op jit(solution)/shard_map/ppermute | solution.py:43
  116.5 15.9 %all-to-all-start.2 = ((f32[16,1,256]{2,1,0:T(1,128)}), f32[16,1,256]{2,1,0:T(1,128)S(1)}, u32[]{:S(2)}, u32[]{:S(2)}) async-start(f32[16,1,256]{2,1,0:T(1,128)} %reshape.21), calls=%async_computation.2 | async-start | bytes 32768 | tf_op jit(solution)/shard_map/all_to_all | solution.py:203
  145.8 16.0 %copy-start.3 = (f32[128,32]{1,0:T(8,128)S(1)}, f32[128,32]{1,0:T(8,128)}, u32[]{:S(2)}) copy-start(f32[128,32]{1,0:T(8,128)} %get-tuple-element.51) | copy-start | bytes 49156
  145.9 23.9 %collective-permute-start.9 = (f32[2,24,1,512]{3,2,1,0:T(1,128)S(1)}, f32[2,24,1,512]{3,2,1,0:T(1,128)S(1)}, u32[]{:S(2)}, u32[]{:S(2)}) collective-permute-start(f32[2,24,1,512]{3,2,1,0:T(1,128)S(1)} %get-tuple-element.37), channel_id=1, source_target_pairs={{0,1},{1,2},{2,3},{3,4},{4,5},{5,6},{6,7},{7,8},{8,9},{9,10},{10,1... | collective-permute-start | bytes 294920 | tf_op jit(solution)/shard_map/ppermute | solution.py:42
  148.4 21.4 %collective-permute-start.10 = (f32[2,24,1,512]{3,2,1,0:T(1,128)S(1)}, f32[2,24,1,512]{3,2,1,0:T(1,128)S(1)}, u32[]{:S(2)}, u32[]{:S(2)}) collective-permute-start(f32[2,24,1,512]{3,2,1,0:T(1,128)S(1)} %get-tuple-element.38), channel_id=1, source_target_pairs={{1,0},{2,1},{3,2},{4,3},{5,4},{6,5},{7,6},{8,7},{9,8},{10,9},{11,1... | collective-permute-start | bytes 294920 | tf_op jit(solution)/shard_map/ppermute | solution.py:43
  153.8 9.5 %collective-permute-start.8 = (f32[2,24,8,1]{3,2,1,0:T(8,128)S(1)}, f32[2,24,8,1]{3,2,1,0:T(8,128)S(1)}, u32[]{:S(2)}, u32[]{:S(2)}) collective-permute-start(f32[2,24,8,1]{3,2,1,0:T(8,128)S(1)} %get-tuple-element.39), channel_id=1, source_target_pairs={{0,16},{16,32},{32,48},{48,64},{64,80},{80,96},{96,112},{1,17},{17... | collective-permute-start | bytes 4616 | tf_op jit(solution)/shard_map/ppermute | solution.py:42
  159.9 10.0 %collective-permute-start.11 = (f32[2,24,8,1]{3,2,1,0:T(8,128)S(1)}, f32[2,24,8,1]{3,2,1,0:T(8,128)S(1)}, u32[]{:S(2)}, u32[]{:S(2)}) collective-permute-start(f32[2,24,8,1]{3,2,1,0:T(8,128)S(1)} %get-tuple-element.40), channel_id=1, source_target_pairs={{16,0},{32,16},{48,32},{64,48},{80,64},{96,80},{112,96},{17,1},{33... | collective-permute-start | bytes 4616 | tf_op jit(solution)/shard_map/ppermute | solution.py:43
  171.3 1.0 copy-start.1
  171.3 1.1 copy-start.2
where the time goes:
time: 177 us; the launch traced here: 175 us
  starting transfers between devices  72.5 us (41%)
  other arithmetic  53 us (30%)
  waiting for transfers between devices  36.8 us (21%)
  local copies, waits for them, and re-layouts  11.8 us (7%)
    mul x1, other arithmetic, closures(): conductivity * jnp.sqrt(saturation)  26.3 us
    ppermute x4, starting transfers between devices, padded_2(): lax.ppermute(last, axis, up)  16.7 us
    all_to_all x1, starting transfers between devices, local(): lax.all_to_all(pressure[0], 'gy', split_axis=1, concat_axis=0, tiled=True)  15.2 us
    another operation x5, other arithmetic, local(): jnp.stack([head, conduct])  14.4 us
    ppermute x4, starting transfers between devices, padded_2(): lax.ppermute(leading, axis, [(b, a) for a, b in up])  14 us
    all_to_all x1, starting transfers between devices, local(): lax.all_to_all(top_conduct, 'gy', split_axis=1, concat_axis=0, tiled=True)  11.5 us
    all_to_all x1, waiting for transfers between devices, local(): lax.all_to_all(top_conduct, 'gy', split_axis=1, concat_axis=0, tiled=True)  11.1 us
    all_to_all x1, waiting for transfers between devices, local(): lax.all_to_all(exchange, 'gy', split_axis=0, concat_axis=1, tiled=True)  9.56 us
  transfers between devices with their start and end apart: 15, of which 6 were waited for; matrix products, arithmetic and copies ran while one was open for 25% of the time, Pallas kernels for 0%

commit v1 on v0

v1 whole, which is shorter than its diff:
```python
import functools

import jax
import jax.numpy as jnp
from jax import lax
from jax.experimental import pallas as pl
from jax.experimental.pallas import tpu as pltpu
from jax.sharding import PartitionSpec as P

MESH = pl.DeviceIdType.MESH
F32 = jnp.float32

STORAGE = 0.01
GRAVITY_STEP = 0.5
SUCTION_FLOOR = 0.01
SLOPE_FLOOR = 0.1
SURFACE_STEP = 0.3
LEAKANCE = 0.5

TILE = 128
ROWS = 8
FIELDS = 5
PARAMS = 6


def lanes():
    return lax.broadcasted_iota(jnp.int32, (ROWS, TILE), 1)


def sublanes():
    return lax.broadcasted_iota(jnp.int32, (ROWS, TILE), 0)


def gather(table, index):
    return jnp.take_along_axis(table, index, axis=1, mode="promise_in_bounds")


def build_tables(tab, kinds):
    lane = lanes()
    rows = []
    for i in range(4):
        row = jnp.zeros((ROWS, TILE), F32)
        for kind in range(kinds):
            row = jnp.where(lane == kind, tab[i, kind], row)
        rows.append(row)
    span, entry, shape, conduct = rows
    shape = jnp.where(lane < kinds, shape, 2.0)
    pore = 1.0 - 1.0 / shape
    expo = 1.0 / (1.0 - pore)
    return (
        -entry,
        expo,
        pore,
        span * pore * expo * entry,
        span,
        2.0 * jnp.sqrt(conduct),
    )


def closures(p, params):
    entry, expo, pore, lead, _, scale = params
    log_scaled = jnp.log(jnp.maximum(entry * p, SUCTION_FLOOR))
    up = expo * log_scaled
    log_sum = jnp.log(1.0 + jnp.exp(up))
    drop = pore * log_sum
    wet = pore * up - drop
    held = jnp.exp(wet)
    capacity = STORAGE + lead * jnp.exp(wet - log_sum)
    fourth = jnp.exp(-0.25 * drop)
    half = fourth * fourth
    root = scale * fourth * (1.0 - held)
    return capacity, half * half, root


def kernel(
    nz, wide, kinds, sizes,
    p_in, k_in, t0_in, t1_in, t2_in, t3_in,
    s0_in, s1_in, s2_in, s3_in, s4_in, s5_in,
    head_out, water_out,
    tab, p, kind, par, cap, sat, root, flow, num,
    row_s, row_r, top_s, top_r, col_s, col_r, tcol_s, tcol_r,
    surf_in, field, below, above,
    down_s, down_r, edge_r, back_s, back_r, source, water,
    sem,
):
    ng, nx, nk = sizes
    tiles = wide // TILE
    per = TILE // 32
    g, x, k = (lax.axis_index(a) for a in ("grp", "gx", "gy"))
    lane, sub = lanes(), sublanes()
    first, last = k == 0, k == nk - 1
    has_n, has_s = g > 0, g < ng - 1
    has_w, has_e = x > 0, x < nx - 1

    names = {}

    def s(name):
        return sem.at[names.setdefault(name, len(names))]

    def at(dg, dx, kk):
        return {"grp": g + dg, "gx": x + dx, "gy": kk}

    def tile(t):
        return slice(t * TILE, (t + 1) * TILE)

    def load(src, dst, name):
        copy = pltpu.make_async_copy(src, dst, s(name))
        copy.start()
        return copy

    table_loads = [
        load(ref, tab.at[i], f"tab{i}")
        for i, ref in enumerate((t0_in, t1_in, t2_in, t3_in))
    ]
    top_loads = [
        load(p_in.at[0:1], p.at[0:1], "p0"),
        load(k_in.at[0:1], kind.at[0:1], "k0"),
    ]
    surf_loads = [
        load(s0_in, surf_in.at[0], "s0"),
        load(s1_in, surf_in.at[1], "s1"),
        load(s2_in, surf_in.at[2], "s2"),
        load(s3_in, surf_in.at[3], "s3"),
    ]
    mask_loads = [
        load(s4_in, water.at[0], "s4"),
        load(s5_in, water.at[1], "s5"),
    ]
    rest_loads = [
        load(p_in.at[1:nz], p.at[1:nz], "p1"),
        load(k_in.at[1:nz], kind.at[1:nz], "k1"),
    ]

    barrier = pltpu.get_barrier_semaphore()

    def greet(device):
        pl.semaphore_signal(barrier, 1, device_id=device, device_id_type=MESH)

    def ring(body):
        def step(i, _):
            body(lax.rem(k + 1 + lax.rem(i + nk // 2 - 1, nk - 1), nk))
            return 0

        lax.fori_loop(0, nk - 1, step, 0)

    def every(body):
        def step(i, _):
            body(i)
            return 0

        lax.fori_loop(0, nk, step, 0)

    col = x * nk + k
    has_l, has_r = col > 0, col < nx * nk - 1
    left = {"gx": jnp.maximum(col - 1, 0) // nk, "gy": lax.rem(jnp.maximum(col - 1, 0), nk)}
    right = {"gx": (col + 1) // nk, "gy": lax.rem(col + 1, nk)}
    row = g * nk + k
    has_u, has_d = row > 0, row < ng * nk - 1
    up = {"grp": jnp.maximum(row - 1, 0) // nk, "gx": x, "gy": lax.rem(jnp.maximum(row - 1, 0), nk)}
    down = {"grp": (row + 1) // nk, "gx": x, "gy": lax.rem(row + 1, nk)}

    ring(lambda kk: greet(at(0, 0, kk)))
    for dg, has in ((-1, has_n), (1, has_s)):
        far = nk - 1 if dg < 0 else 0

        @pl.when(has)
        def _():
            greet(at(dg, 0, far))
            greet(at(dg, 0, k))

            @pl.when(has_l)
            def _():
                greet({"grp": g + dg, **left})

            @pl.when(has_r)
            def _():
                greet({"grp": g + dg, **right})

            @pl.when(first & has_w)
            def _():
                greet(at(dg, -1, far))

            @pl.when(last & has_e)
            def _():
                greet(at(dg, 1, far))

    @pl.when(has_w)
    def _():
        greet(at(0, -1, k))

        @pl.when(first)
        def _():
            every(lambda kk: greet(at(0, -1, kk)))

    @pl.when(has_e)
    def _():
        greet(at(0, 1, k))

        @pl.when(last)
        def _():
            every(lambda kk: greet(at(0, 1, kk)))

    def one(flag):
        return flag.astype(jnp.int32)

    rows_to = one(has_n) + one(has_s)
    cols_to = one(has_w) + one(has_e)
    corner = one(first & has_n) + one(last & has_s)
    expected = (
        (nk - 1)
        + corner * nk
        + rows_to * (1 + one(has_l) + one(has_r))
        + 2 * cols_to
        + corner * cols_to
    )

    zero = jnp.zeros((ROWS, TILE), F32)

    def clear(ref, rows):
        for r in range(0, rows, ROWS):
            for c in range(0, ref.shape[-1], TILE):
                ref[r : r + ROWS, c : c + TILE] = zero

    for t in range(tiles):
        for ph in range(2):
            for z in (0, nz + 1):
                root[ph, z, :, tile(t)] = zero
                flow[ph, z, :, tile(t)] = zero

    for d, has, has_g, ref in ((0, has_u, has_n, above), (1, has_d, has_s, below)):

        @pl.when(jnp.logical_not(has))
        def _():
            for ph in range(2):
                for i in range(2):
                    for t in range(tiles):
                        clear(row_r.at[ph, d, i, t], nz)
            clear(top_r.at[d], ROWS)

        @pl.when(jnp.logical_not(has_g))
        def _():
            for f in range(FIELDS):
                clear(ref.at[f], 48)
            off = 248 if d == 0 else 128
            clear(down_r.at[off : off + ROWS], ROWS)

        @pl.when(has_g & jnp.logical_not(has_r))
        def _():
            for f in range(FIELDS):
                ref[f, 32:40, :] = zero

        @pl.when(has_g & jnp.logical_not(has_l))
        def _():
            for f in range(FIELDS):
                ref[f, 40:48, :] = zero

    for d, has in ((0, has_w), (1, has_e)):

        @pl.when(jnp.logical_not(has))
        def _():
            for ph in range(2):
                col_r[ph, d] = zero
            tcol_r[d] = zero

    for d, has in ((0, has_r), (1, has_l)):

        @pl.when(jnp.logical_not(has))
        def _():
            for f in range(FIELDS):
                field[f, 32 + 8 * d : 40 + 8 * d, 0:TILE] = zero

    gets_edge = (first & has_w) | (last & has_e)

    @pl.when(jnp.logical_not(gets_edge))
    def _():
        clear(edge_r.at[0:TILE], TILE)

    for off, has in ((128, has_s), (248, has_n)):

        @pl.when(jnp.logical_not(gets_edge & has))
        def _():
            clear(edge_r.at[off : off + ROWS], ROWS)

    for c in table_loads:
        c.wait()
    tables = build_tables(tab, kinds)

    def layer_params(z, t):
        index = kind[z, :, tile(t)]
        return [gather(table, index) for table in tables]

    def put_row(dst_first, dst_last, i, z, t, value):
        dst_first[i, t, pl.ds(z, 1), :] = value[0:1, :]
        dst_last[i, t, pl.ds(z, 1), :] = value[7:8, :]

    def shift_to(value, frm, to):
        return pltpu.roll(value, lax.rem(to - frm + TILE, TILE), 1)

    def put_cols(packs, z, q0, r0, q1, r1):
        west, east = packs
        west = jnp.where(lane == z, shift_to(q0, 0, z), west)
        west = jnp.where(lane == z + 64, shift_to(r0, 0, z + 64), west)
        east = jnp.where(lane == z, shift_to(q1, TILE - 1, z), east)
        east = jnp.where(lane == z + 64, shift_to(r1, TILE - 1, z + 64), east)
        return west, east

    def first_closures(z, packs):
        ends = []
        for t in range(tiles):
            params = layer_params(z, t)
            for i in range(PARAMS):
                par[i, z, :, tile(t)] = params[i]
            pz = p[z, :, tile(t)]
            c, se, q = closures(pz, params)
            r = q * pz
            cap[z, :, tile(t)] = c
            sat[z, :, tile(t)] = se
            root[0, z + 1, :, tile(t)] = q
            flow[0, z + 1, :, tile(t)] = r
            put_row(row_s.at[0, 0], row_s.at[0, 1], 0, z, t, q)
            put_row(row_s.at[0, 0], row_s.at[0, 1], 1, z, t, r)
            ends.append((q, r))
        return put_cols(packs, z, *ends[0], *ends[-1])

    for c in top_loads:
        c.wait()
    packs = first_closures(0, (zero, zero))

    tops = [p[0, :, tile(t)] for t in range(tiles)]
    halves = [jnp.square(root[0, 1, :, tile(t)]) * 0.125 for t in range(tiles)]

    def turn(v, by):
        by %= TILE
        return pltpu.roll(v, by, 1) if by else v

    def cut(parts, kk, base):
        t, o = divmod(kk * 32, TILE)
        out = turn(parts[t], base - o)
        before = parts[t] if o else parts[max(t - 1, 0)]
        out = jnp.where(
            (lane >= base + 38) & (lane < base + 40), turn(before, base + 40 - o), out
        )
        if o + 32 == TILE and t + 1 < tiles:
            after = turn(parts[t + 1], base + 32)
            out = jnp.where((lane >= base + 32) & (lane < base + 34), after, out)
        return out

    for kk in range(nk):
        down_s[kk] = jnp.where(lane < 64, cut(tops, kk, 0), cut(halves, kk, 64))
    down_s[nk] = jnp.where(lane < 64, turn(tops[-1], 40), turn(halves[-1], 104))
    down_s[nk + 1] = jnp.where(lane < 64, turn(tops[0], 32), turn(halves[0], 96))
    mine = pl.multiple_of(k * ROWS, ROWS)
    down_r[pl.ds(mine, ROWS), :] = down_s[k]

    pl.semaphore_wait(barrier, expected)

    pending = []

    def send(src, dst, name, device, when=None, keep=True):
        copy = pltpu.make_async_remote_copy(
            src_ref=src,
            dst_ref=dst,
            send_sem=s(name + "_s"),
            recv_sem=s(name + "_r"),
            device_id=device,
            device_id_type=MESH,
        )
        if when is None:
            copy.start()
        else:
            pl.when(when)(copy.start)
        if keep:
            pending.append((copy, when))
        return copy

    def drain(ref, name, when=None):
        wait = pltpu.make_async_copy(ref, ref, s(name)).wait
        if when is None:
            wait()
        else:
            pl.when(when)(wait)

    ring(
        lambda kk: send(
            down_s.at[kk], down_r.at[pl.ds(mine, ROWS)], "down", at(0, 0, kk), keep=False
        )
    )
    for dg, far, has, slot in ((1, last, has_s, 248), (-1, first, has_n, 128)):

        @pl.when(far & has)
        def _():
            every(
                lambda kk: send(
                    down_s.at[kk], down_r.at[slot : slot + ROWS], f"down{slot}", at(dg, 0, kk),
                    keep=False,
                )
            )

        for dx, kk, has_x, i in ((1, 0, has_e, nk), (-1, nk - 1, has_w, nk + 1)):
            send(
                down_s.at[i], edge_r.at[slot : slot + ROWS], f"edge{slot}{dx}",
                at(dg, dx, kk), far & has & has_x,
            )
    for dx, kk, has_x, i in ((1, 0, has_e, nk), (-1, nk - 1, has_w, nk + 1)):
        send(
            down_s.at[i], edge_r.at[pl.ds(mine, ROWS)], f"edge{dx}", at(0, dx, kk), has_x
        )

    for c in surf_loads + mask_loads:
        c.wait()
    field[0, 0:32, 0:TILE] = surf_in[0]
    field[1, 0:32, 0:TILE] = surf_in[1]
    field[2, 0:32, 0:TILE] = jnp.sqrt((1.0 + water[1].astype(F32)) / surf_in[2])
    field[3, 0:32, 0:TILE] = surf_in[3]
    field[4, 0:32, 0:TILE] = water[0].astype(F32)

    def own(a, b):
        return field.at[:, a:b, 0:TILE]

    send(own(24, 32), own(40, 48), "right", {"grp": g, **right}, has_r)
    send(own(0, 8), own(32, 40), "left", {"grp": g, **left}, has_l)
    for dg, has, ref, n in ((1, has_s, above, "s"), (-1, has_n, below, "n")):
        send(own(0, 32), ref.at[:, 0:32], "line" + n, at(dg, 0, k), has)
        send(own(24, 32), ref.at[:, 40:48], "right" + n, {"grp": g + dg, **right}, has & has_r)
        send(own(0, 8), ref.at[:, 32:40], "left" + n, {"grp": g + dg, **left}, has & has_l)

    for c in rest_loads:
        c.wait()
    packs = lax.fori_loop(1, nz, first_closures, packs)
    col_s[0, 0], col_s[0, 1] = packs

    def send_soil(ph):
        send(row_s.at[ph, 1], row_r.at[ph, 0], f"row{ph}d", down, has_d)
        send(row_s.at[ph, 0], row_r.at[ph, 1], f"row{ph}u", up, has_u)
        send(col_s.at[ph, 1], col_r.at[ph, 0], f"col{ph}e", at(0, 1, k), has_e)
        send(col_s.at[ph, 0], col_r.at[ph, 1], f"col{ph}w", at(0, -1, k), has_w)

    def wait_soil(ph):
        drain(row_r.at[ph, 0], f"row{ph}d_r", has_u)
        drain(row_r.at[ph, 1], f"row{ph}u_r", has_d)
        drain(col_r.at[ph, 0], f"col{ph}e_r", has_w)
        drain(col_r.at[ph, 1], f"col{ph}w_r", has_e)

    send_soil(0)

    drain(own(40, 48), "right_r", has_l)
    drain(own(32, 40), "left_r", has_r)
    for has, ref, n in ((has_n, above, "s"), (has_s, below, "n")):
        drain(ref.at[:, 0:32], "line" + n + "_r", has)
        drain(ref.at[:, 40:48], "right" + n + "_r", has & has_l)
        drain(ref.at[:, 32:40], "left" + n + "_r", has & has_r)
    side = lax.broadcasted_iota(jnp.int32, (48, TILE), 1) < 64
    full = []
    for f in range(FIELDS):
        full.append(
            jnp.concatenate(
                [field[f, :, 0:TILE], jnp.where(side, below[f], above[f])], axis=1
            )
        )
    w0, level, bed, rain, land = full

    def next_of(v, axis):
        return pltpu.roll(v, v.shape[axis] - 1, axis)

    def prev_of(v, axis):
        return pltpu.roll(v, 1, axis)

    faces = [bed * next_of(bed, axis) for axis in (0, 1)]

    def outflow(w):
        carried = jnp.exp((5.0 / 3.0) * jnp.log(jnp.maximum(w, 1e-30)))
        surface = level + w
        total = None
        for axis in (0, 1):
            slope = surface - next_of(surface, axis)
            upwind = jnp.where(slope >= 0, carried, next_of(carried, axis))
            flux = faces[axis] * upwind * slope * lax.rsqrt(
                jnp.maximum(jnp.abs(slope), SLOPE_FLOOR)
            )
            net = flux - prev_of(flux, axis)
            total = net if total is None else total + net
        return total

    out0 = outflow(w0)

    drain(down_s.at[0 : nk - 1], "down_r")
    drain(down_s.at[0], "down128_r", has_s)
    drain(down_s.at[0], "down248_r", has_n)
    for dx, gets in ((1, first & has_w), (-1, last & has_e)):
        drain(edge_r.at[0:TILE], f"edge{dx}_r", gets)
        drain(down_s.at[0], f"edge128{dx}_r", gets & has_s)
        drain(down_s.at[0], f"edge248{dx}_r", gets & has_n)

    tall = lax.broadcasted_iota(jnp.int32, (TILE, TILE), 0)
    wide_lane = lax.broadcasted_iota(jnp.int32, (TILE, TILE), 1) & 63
    low = jnp.where(first, 38, 32)
    use_edge = (wide_lane >= low) & (wide_lane < low + 2) & (first | last)

    def received(a):
        rows = jnp.where(use_edge, edge_r[a : a + TILE, :], down_r[a : a + TILE, :])
        if a:
            rows = jnp.where((tall < ROWS) | (tall >= TILE - ROWS), rows, 0.0)
        return rows.T

    main, rim = received(0), received(TILE)

    def pick(a):
        body = [main[a : a + 32], rim[a : a + 32]]
        halo = [main[a + 32 : a + 40], rim[a + 32 : a + 40]]
        body, halo = (jnp.concatenate(v, axis=1) for v in (body, halo))
        return jnp.concatenate([body, halo, halo], axis=0)

    top = pick(0)
    leak = land * pick(64)

    def advance(w, out):
        rate = leak * (w - top)
        return jnp.maximum(w + SURFACE_STEP * (rain - rate - out), 0.0), rate

    w1, rate0 = advance(w0, out0)
    w2, rate1 = advance(w1, outflow(w1))
    rate2 = leak * (w2 - top)
    exchange = SURFACE_STEP * (rate0 + rate1 + rate2)
    square = jnp.concatenate([exchange[0:32, 0:TILE], jnp.zeros((96, TILE), F32)], axis=0)
    back_s[...] = square.T.reshape(nk, ROWS, TILE)
    back_r[k] = back_s[k]
    ring(
        lambda kk: send(back_s.at[kk], back_r.at[k], "back", at(0, 0, kk), keep=False)
    )
    w3, _ = advance(w2, outflow(w2))
    surf_in[0] = w3[0:32, 0:TILE]
    stores = [load(surf_in.at[0], water_out, "water")]

    def sums(ph, z, t, halo_rows, halo_cols):
        both = []
        for i, ref in enumerate((root, flow)):
            mid = ref[ph, z + 1, :, tile(t)]
            total = ref[ph, z, :, tile(t)] + ref[ph, z + 2, :, tile(t)]
            above_row, below_row = halo_rows[0][i], halo_rows[1][i]
            total += jnp.where(sub == 0, above_row, pltpu.roll(mid, 1, 0))
            total += jnp.where(sub == ROWS - 1, below_row, pltpu.roll(mid, ROWS - 1, 0))
            if t > 0:
                west = pltpu.roll(ref[ph, z + 1, :, tile(t - 1)], 1, 1)
            else:
                west = halo_cols[0][i]
            if t + 1 < tiles:
                east = pltpu.roll(ref[ph, z + 1, :, tile(t + 1)], TILE - 1, 1)
            else:
                east = halo_cols[1][i]
            total += jnp.where(lane == 0, west, pltpu.roll(mid, 1, 1))
            total += jnp.where(lane == TILE - 1, east, pltpu.roll(mid, TILE - 1, 1))
            both.append(total)
        q, r = both
        r += GRAVITY_STEP * (root[ph, z, :, tile(t)] - root[ph, z + 2, :, tile(t)])
        return q, r

    def plain_halo(ph, z):
        def rows(t):
            return [
                [row_r[ph, d, i, t, pl.ds(z, 1), :] for i in range(2)] for d in range(2)
            ]

        cols = [
            [shift_to(col_r[ph, d], z + 64 * i, (TILE - 1) * d) for i in range(2)]
            for d in range(2)
        ]
        return rows, cols

    def top_halo():
        def rows(t):
            return [[top_r[d, i : i + 1, tile(t)] for i in range(2)] for d in range(2)]

        cols = [
            [shift_to(tcol_r[d], 64 * i, (TILE - 1) * d) for i in range(2)]
            for d in range(2)
        ]
        return rows, cols

    def sweep(ph, z, t, halo, base, weight, extra):
        rows, cols = halo
        q, r = sums(ph, z, t, rows(t), cols)
        own_root = root[ph, z + 1, :, tile(t)]
        above_line = base + own_root * r
        if extra is not None:
            above_line += extra
        return above_line / (weight + own_root * q)

    def second_closures(z, packs, extras=None):
        halo = plain_halo(0, z)
        ends = []
        for t in range(tiles):
            c0 = cap[z, :, tile(t)]
            extra = None if extras is None else extras[t]
            head = sweep(0, z, t, halo, c0 * p[z, :, tile(t)], c0, extra)
            params = [par[i, z, :, tile(t)] for i in range(PARAMS)]
            c, se, q = closures(head, params)
            r = q * head
            ends.append((c, se, q, r, head, params[4]))
        for t in range(tiles):
            c, se, q, r, head, span = ends[t]
            gap = span * (se - sat[z, :, tile(t)])
            cap[z, :, tile(t)] = c
            num[z, :, tile(t)] = c * head - gap
            root[1, z + 1, :, tile(t)] = q
            flow[1, z + 1, :, tile(t)] = r
            if extras is None:
                put_row(row_s.at[1, 0], row_s.at[1, 1], 0, z, t, q)
                put_row(row_s.at[1, 0], row_s.at[1, 1], 1, z, t, r)
            else:
                for i, v in ((0, q), (1, r)):
                    top_s[0, i : i + 1, tile(t)] = v[0:1, :]
                    top_s[1, i : i + 1, tile(t)] = v[7:8, :]
        return put_cols(packs, z, *ends[0][2:4], *ends[-1][2:4])

    for t in range(tiles):
        for d in range(2):
            top_s[d, :, tile(t)] = zero
            for i in range(2):
                row_s[1, d, i, t, 0:ROWS, :] = zero
    wait_soil(0)
    packs = lax.fori_loop(1, nz, second_closures, (zero, zero))
    col_s[1, 0], col_s[1, 1] = packs
    send_soil(1)

    drain(down_s.at[0 : nk - 1], "back_r")
    extras = []
    for t in range(tiles):
        v = back_r[per * t]
        for i in range(1, per):
            v = jnp.where(lane >= 32 * i, turn(back_r[per * t + i], 32 * i), v)
        source[:, tile(t)] = v
        extras.append(v)
    tcol_s[0], tcol_s[1] = second_closures(0, (zero, zero), extras)
    send(top_s.at[1], top_r.at[0], "topd", down, has_d)
    send(top_s.at[0], top_r.at[1], "topu", up, has_u)
    send(tcol_s.at[1], tcol_r.at[0], "tope", at(0, 1, k), has_e)
    send(tcol_s.at[0], tcol_r.at[1], "topw", at(0, -1, k), has_w)

    wait_soil(1)

    def last_sweep(z, halo, extra=False):
        for t in range(tiles):
            more = source[:, tile(t)] if extra else None
            p[z, :, tile(t)] = sweep(
                1, z, t, halo, num[z, :, tile(t)], cap[z, :, tile(t)], more
            )

    def last_step(z, carry):
        last_sweep(z, plain_halo(1, z))
        return carry

    lax.fori_loop(1, nz, last_step, 0)
    stores.append(load(p.at[1:nz], head_out.at[1:nz], "head1"))
    drain(top_r.at[0], "topd_r", has_u)
    drain(top_r.at[1], "topu_r", has_d)
    drain(tcol_r.at[0], "tope_r", has_w)
    drain(tcol_r.at[1], "topw_r", has_e)
    last_sweep(0, top_halo(), True)
    stores.append(load(p.at[0:1], head_out.at[0:1], "head0"))

    drain(down_s.at[0 : nk - 1], "down_s")
    drain(down_s.at[0 : nk - 1], "back_s")
    drain(down_s.at[0:nk], "down248_s", last & has_s)
    drain(down_s.at[0:nk], "down128_s", first & has_n)
    for copy, when in pending:
        if when is None:
            copy.wait_send()
        else:
            pl.when(when)(copy.wait_send)
    for c in stores:
        c.wait()


def solution(mesh):
    sizes = tuple(mesh.shape[a] for a in ("grp", "gx", "gy"))
    nk = sizes[2]

    def local(
        pressure, soil_class, capacity_range, inverse_entry, shape_index, conductivity,
        depth, elevation, roughness, rain, land_mask, channel_mask,
    ):
        nz, _, wide = pressure.shape
        kinds = capacity_range.shape[0]
        hbm = pl.BlockSpec(memory_space=pl.ANY)
        soil = (nz, ROWS, wide)
        vmem = pltpu.VMEM
        head, water = pl.pallas_call(
            functools.partial(kernel, nz, wide, kinds, sizes),
            out_shape=(
                jax.ShapeDtypeStruct(pressure.shape, F32),
                jax.ShapeDtypeStruct(depth.shape[::-1], F32),
            ),
            in_specs=[hbm] * 12,
            out_specs=(hbm, hbm),
            scratch_shapes=[
                pltpu.SMEM((4, kinds), F32),
                vmem(soil, F32),
                vmem(soil, jnp.int32),
                vmem((PARAMS, *soil), F32),
                vmem(soil, F32),
                vmem(soil, F32),
                vmem((2, nz + 2, ROWS, wide), F32),
                vmem((2, nz + 2, ROWS, wide), F32),
                vmem(soil, F32),
                vmem((2, 2, 2, wide // TILE, nz, TILE), F32),
                vmem((2, 2, 2, wide // TILE, nz, TILE), F32),
                vmem((2, ROWS, wide), F32),
                vmem((2, ROWS, wide), F32),
                vmem((2, 2, ROWS, TILE), F32),
                vmem((2, 2, ROWS, TILE), F32),
                vmem((2, ROWS, TILE), F32),
                vmem((2, ROWS, TILE), F32),
                vmem((4, 32, TILE), F32),
                vmem((FIELDS, 48, 2 * TILE), F32),
                vmem((FIELDS, 48, TILE), F32),
                vmem((FIELDS, 48, TILE), F32),
                vmem((nk + 2, ROWS, TILE), F32),
                vmem((2 * TILE, TILE), F32),
                vmem((2 * TILE, TILE), F32),
                vmem((nk, ROWS, TILE), F32),
                vmem((nk, ROWS, TILE), F32),
                vmem((ROWS, wide), F32),
                vmem((2, 32, TILE), jnp.int32),
                pltpu.SemaphoreType.DMA((100,)),
            ],
            compiler_params=pltpu.CompilerParams(
                collective_id=0, has_side_effects=True, vmem_limit_bytes=48 * 1024 * 1024
            ),
        )(
            pressure, soil_class, capacity_range, inverse_entry, shape_index, conductivity,
            depth.T, elevation.T, roughness.T, rain.T, land_mask.T, channel_mask.T,
        )
        return head, water.T

    tile = P(None, ("grp", "gy"), "gx")
    flat = P("grp", ("gx", "gy"))
    return jax.shard_map(
        local,
        mesh=mesh,
        in_specs=(tile, tile, P(), P(), P(), P()) + (flat,) * 6,
        out_specs=(tile, flat),
        check_vma=False,
    )
```

time: 177 us -> 50.7 us (0.29)
  the two profiles are of different devices: /device:TPU:14 before, /device:TPU:1 now
where the time goes in v1:
time: 50.7 us; the launch traced here: 49.7 us
  Pallas kernels  40.7 us (80%)
  local copies, waits for them, and re-layouts  8.32 us (16%)
  between operations  0.69 us (1%)
    pallas_call x1, Pallas kernels, local(): pl.pallas_call(functools.partial(kernel, nz, wide, kinds, sizes), out_sha...  40.7 us
    unnamed x26, local copies, waits for them, and re-layouts  8.32 us

profile of v1, /device:TPU:1, one launch (start us, length us, event | category | flops | bytes accessed | tf_op | source)
XLA Modules:
  0.0 49.7 jit_solution(2856101781115863123)
XLA Ops:
  0.6 0.0 copy-start.11
  0.6 0.0 copy-start.8
  0.7 0.0 copy-start.9
  0.7 0.0 copy-start.10
  0.7 0.6 %copy-done.11 = f32[12]{0:T(128)S(1)} copy-done((f32[12]{0:T(128)S(1)}, f32[12]{0:T(128)}, u32[]{:S(2)}) %copy-start.11) | copy-done | bytes 72
  1.3 0.0 copy-done.8
  1.3 0.0 copy-done.9
  1.3 0.0 copy-done.10
  1.3 0.0 copy-start
  1.3 1.0 %copy-done = f32[24,8,512]{2,1,0:T(8,128)S(1)} copy-done((f32[24,8,512]{2,1,0:T(8,128)S(1)}, f32[24,8,512]{2,1,0:T(8,128)}, u32[]{:S(2)}) %copy-start) | copy-done | bytes 393240
  2.3 0.0 copy-start.1
  2.3 1.0 %copy-done.1 = s32[24,8,512]{2,1,0:T(8,128)S(1)} copy-done((s32[24,8,512]{2,1,0:T(8,128)S(1)}, s32[24,8,512]{2,1,0:T(8,128)}, u32[]{:S(2)}) %copy-start.1) | copy-done | bytes 393240
  3.3 0.0 copy-start.2
  3.3 0.7 %copy-done.2 = f32[128,32]{0,1:T(8,128)S(1)} copy-done((f32[128,32]{0,1:T(8,128)S(1)}, f32[128,32]{0,1:T(8,128)}, u32[]{:S(2)}) %copy-start.2) | copy-done | bytes 16408
  4.0 0.0 copy-start.3
  4.1 0.7 %copy-done.3 = f32[128,32]{0,1:T(8,128)S(1)} copy-done((f32[128,32]{0,1:T(8,128)S(1)}, f32[128,32]{0,1:T(8,128)}, u32[]{:S(2)}) %copy-start.3) | copy-done | bytes 16408
  4.8 0.0 copy-start.4
  4.8 0.7 %copy-done.4 = f32[128,32]{0,1:T(8,128)S(1)} copy-done((f32[128,32]{0,1:T(8,128)S(1)}, f32[128,32]{0,1:T(8,128)}, u32[]{:S(2)}) %copy-start.4) | copy-done | bytes 16408
  5.5 0.0 copy-start.5
  5.5 0.7 %copy-done.5 = f32[128,32]{0,1:T(8,128)S(1)} copy-done((f32[128,32]{0,1:T(8,128)S(1)}, f32[128,32]{0,1:T(8,128)}, u32[]{:S(2)}) %copy-start.5) | copy-done | bytes 16408
  6.2 0.0 copy-start.6
  6.2 0.7 %copy-done.6 = s32[128,32]{0,1:T(8,128)S(1)} copy-done((s32[128,32]{0,1:T(8,128)S(1)}, s32[128,32]{0,1:T(8,128)}, u32[]{:S(2)}) %copy-start.6) | copy-done | bytes 16408
  6.9 0.0 copy-start.7
  6.9 0.7 %copy-done.7 = s32[128,32]{0,1:T(8,128)S(1)} copy-done((s32[128,32]{0,1:T(8,128)S(1)}, s32[128,32]{0,1:T(8,128)}, u32[]{:S(2)}) %copy-start.7) | copy-done | bytes 16408
  7.6 40.7 %shard_map.131 = (f32[24,8,512]{2,1,0:T(8,128)S(1)}, f32[32,128]{1,0:T(8,128)S(1)}) custom-call(f32[24,8,512]{2,1,0:T(8,128)S(1)} %copy-done, s32[24,8,512]{2,1,0:T(8,128)S(1)} %copy-done.1, f32[12]{0:T(128)S(1)} %copy-done.8, f32[12]{0:T(128)S(1)} %copy-done.9, f32[12]{0:T(128)S(1)} %copy-done.10, f32[12]{0:T(128)S(1)} %copy-done.11, ...), custom_call_target="tpu_custom_call" | custom-call | tf_op jit(solution)/shard_map/pallas_call | solution.py:687
  48.3 0.7 %copy.16 = f32[24,8,512]{2,1,0:T(8,128)} copy(f32[24,8,512]{2,1,0:T(8,128)S(1)} %get-tuple-element.8) | data formatting | bytes 786432
  49.1 0.6 %copy.17 = f32[128,32]{0,1:T(8,128)} copy(f32[128,32]{0,1:T(8,128)S(1)} %bitcast.13) | data formatting | bytes 32768
Async XLA Ops:
  0.6 0.7 %copy-start.11 = (f32[12]{0:T(128)S(1)}, f32[12]{0:T(128)}, u32[]{:S(2)}) copy-start(f32[12]{0:T(128)} %t3_in.1) | copy-start | bytes 148
  0.6 0.7 %copy-start.8 = (f32[12]{0:T(128)S(1)}, f32[12]{0:T(128)}, u32[]{:S(2)}) copy-start(f32[12]{0:T(128)} %t0_in.1) | copy-start | bytes 148
  0.7 0.7 %copy-start.9 = (f32[12]{0:T(128)S(1)}, f32[12]{0:T(128)}, u32[]{:S(2)}) copy-start(f32[12]{0:T(128)} %t1_in.1) | copy-start | bytes 148
  0.7 0.7 %copy-start.10 = (f32[12]{0:T(128)S(1)}, f32[12]{0:T(128)}, u32[]{:S(2)}) copy-start(f32[12]{0:T(128)} %t2_in.1) | copy-start | bytes 148
  1.3 1.0 %copy-start = (f32[24,8,512]{2,1,0:T(8,128)S(1)}, f32[24,8,512]{2,1,0:T(8,128)}, u32[]{:S(2)}) copy-start(f32[24,8,512]{2,1,0:T(8,128)} %p_in.1) | copy-start | bytes 1179652
  2.3 1.0 %copy-start.1 = (s32[24,8,512]{2,1,0:T(8,128)S(1)}, s32[24,8,512]{2,1,0:T(8,128)}, u32[]{:S(2)}) copy-start(s32[24,8,512]{2,1,0:T(8,128)} %k_in.1) | copy-start | bytes 1179652
  3.3 0.7 %copy-start.2 = (f32[128,32]{0,1:T(8,128)S(1)}, f32[128,32]{0,1:T(8,128)}, u32[]{:S(2)}) copy-start(f32[128,32]{0,1:T(8,128)} %param.18) | copy-start | bytes 49156
  4.0 0.7 %copy-start.3 = (f32[128,32]{0,1:T(8,128)S(1)}, f32[128,32]{0,1:T(8,128)}, u32[]{:S(2)}) copy-start(f32[128,32]{0,1:T(8,128)} %param.19) | copy-start | bytes 49156
  4.8 0.7 %copy-start.4 = (f32[128,32]{0,1:T(8,128)S(1)}, f32[128,32]{0,1:T(8,128)}, u32[]{:S(2)}) copy-start(f32[128,32]{0,1:T(8,128)} %param.20) | copy-start | bytes 49156
  5.5 0.7 %copy-start.5 = (f32[128,32]{0,1:T(8,128)S(1)}, f32[128,32]{0,1:T(8,128)}, u32[]{:S(2)}) copy-start(f32[128,32]{0,1:T(8,128)} %param.21) | copy-start | bytes 49156
  6.2 0.7 %copy-start.6 = (s32[128,32]{0,1:T(8,128)S(1)}, s32[128,32]{0,1:T(8,128)}, u32[]{:S(2)}) copy-start(s32[128,32]{0,1:T(8,128)} %param.22) | copy-start | bytes 49156
  6.9 0.7 %copy-start.7 = (s32[128,32]{0,1:T(8,128)S(1)}, s32[128,32]{0,1:T(8,128)}, u32[]{:S(2)}) copy-start(s32[128,32]{0,1:T(8,128)} %param.23) | copy-start | bytes 49156

commit v2 on v1

--- a/solution.py
+++ b/solution.py
@@ -724,7 +724,7 @@
                 pltpu.SemaphoreType.DMA((100,)),
             ],
             compiler_params=pltpu.CompilerParams(
-                collective_id=0, has_side_effects=True, vmem_limit_bytes=48 * 1024 * 1024
+                collective_id=0, has_side_effects=True, vmem_limit_bytes=60 * 1024 * 1024
             ),
         )(
             pressure, soil_class, capacity_range, inverse_entry, shape_index, conductivity,

time: 50.7 us -> 44 us (0.87); the launches traced: 49.7 us -> 43.6 us
  local copies, waits for them, and re-layouts: 8.32 us -> 2.38 us
    unnamed x26 -> x4, local copies, waits for them, and re-layouts: 8.32 us -> 2.38 us
where the time goes in v2:
time: 44 us; the launch traced here: 43.6 us
  Pallas kernels  40.5 us (92%)
  local copies, waits for them, and re-layouts  2.38 us (5%)
  between operations  0.65 us (1%)
    pallas_call x1, Pallas kernels, local(): pl.pallas_call(functools.partial(kernel, nz, wide, kinds, sizes), out_sha...  40.5 us
    unnamed x4, local copies, waits for them, and re-layouts  2.38 us

profile of v2, /device:TPU:1, one launch (start us, length us, event | category | flops | bytes accessed | tf_op | source)
XLA Modules:
  0.0 43.6 jit_solution(6333099732448492556)
XLA Ops:
  0.6 40.5 %shard_map.131 = (f32[24,8,512]{2,1,0:T(8,128)}, f32[32,128]{1,0:T(8,128)}) custom-call(f32[24,8,512]{2,1,0:T(8,128)} %p_in.1, s32[24,8,512]{2,1,0:T(8,128)} %k_in.1, f32[12]{0:T(128)} %t0_in.1, f32[12]{0:T(128)} %t1_in.1, f32[12]{0:T(128)} %t2_in.1, f32[12]{0:T(128)} %t3_in.1, f32[32,128]{1,0:T(8,128)} %bitcast.7, f32[32,128]{1,0:T(8,128)} %bitcast.8, ...), custom_call_target="tpu_custom_call" | custom-call | tf_op jit(solution)/shard_map/pallas_call | solution.py:687
  41.2 0.0 copy-start
  41.2 1.8 %copy.16 = f32[24,8,512]{2,1,0:T(8,128)} copy(f32[24,8,512]{2,1,0:T(8,128)} %get-tuple-element.8) | data formatting | bytes 786432
  43.0 0.0 copy-done
  43.0 0.6 %copy.17 = f32[128,32]{0,1:T(8,128)} copy(f32[128,32]{0,1:T(8,128)S(1)} %bitcast.13) | data formatting | bytes 32768
Async XLA Ops:
  41.2 1.8 %copy-start = (f32[32,128]{1,0:T(8,128)S(1)}, f32[32,128]{1,0:T(8,128)}, u32[]{:S(2)}) copy-start(f32[32,128]{1,0:T(8,128)} %get-tuple-element.5) | copy-start | bytes 49156

commit v3 on v2

--- a/solution.py
+++ b/solution.py
@@ -80,7 +80,7 @@
     tab, p, kind, par, cap, sat, root, flow, num,
     row_s, row_r, top_s, top_r, col_s, col_r, tcol_s, tcol_r,
     surf_in, field, below, above,
-    down_s, down_r, edge_r, back_s, back_r, source, water,
+    down_s, down_r, edge_r, under_s, under_r, rim_s, rim_r, source, water,
     sem,
 ):
     ng, nx, nk = sizes
@@ -167,6 +167,11 @@
         def _():
             greet(at(dg, 0, far))
             greet(at(dg, 0, k))
+            ends = first if dg < 0 else last
+
+            @pl.when(ends)
+            def _():
+                every(lambda kk: greet(at(dg, 0, kk)))
 
             @pl.when(has_l)
             def _():
@@ -184,9 +189,18 @@
             def _():
                 greet(at(dg, 1, far))
 
+            @pl.when(ends & has_w)
+            def _():
+                greet(at(dg, -1, nk - 1))
+
+            @pl.when(ends & has_e)
+            def _():
+                greet(at(dg, 1, 0))
+
     @pl.when(has_w)
     def _():
         greet(at(0, -1, k))
+        greet(at(0, -1, nk - 1))
 
         @pl.when(first)
         def _():
@@ -195,6 +209,7 @@
     @pl.when(has_e)
     def _():
         greet(at(0, 1, k))
+        greet(at(0, 1, 0))
 
         @pl.when(last)
         def _():
@@ -206,12 +221,14 @@
     rows_to = one(has_n) + one(has_s)
     cols_to = one(has_w) + one(has_e)
     corner = one(first & has_n) + one(last & has_s)
+    side = one(first & has_w) + one(last & has_e)
     expected = (
         (nk - 1)
         + corner * nk
-        + rows_to * (1 + one(has_l) + one(has_r))
+        + rows_to * (2 + one(has_l) + one(has_r))
         + 2 * cols_to
         + corner * cols_to
+        + side * (nk + rows_to)
     )
 
     zero = jnp.zeros((ROWS, TILE), F32)
@@ -280,6 +297,25 @@
         @pl.when(jnp.logical_not(gets_edge & has))
         def _():
             clear(edge_r.at[off : off + ROWS], ROWS)
+
+    for slot, has in ((nk, has_e), (nk + 1, has_w)):
+
+        @pl.when(jnp.logical_not(has))
+        def _():
+            clear(under_r.at[slot], 2 * ROWS)
+
+    gets_rim = (first & has_n) | (last & has_s)
+
+    @pl.when(jnp.logical_not(gets_rim))
+    def _():
+        for j in range(nk):
+            rim_r[j] = zero
+
+    for slot, has in ((nk, has_e), (nk + 1, has_w)):
+
+        @pl.when(jnp.logical_not(gets_rim & has))
+        def _():
+            rim_r[slot] = zero
 
     for c in table_loads:
         c.wait()
@@ -352,8 +388,6 @@
     mine = pl.multiple_of(k * ROWS, ROWS)
     down_r[pl.ds(mine, ROWS), :] = down_s[k]
 
-    pl.semaphore_wait(barrier, expected)
-
     pending = []
 
     def send(src, dst, name, device, when=None, keep=True):
@@ -380,6 +414,81 @@
         else:
             pl.when(when)(wait)
 
+    for c in surf_loads + mask_loads:
+        c.wait()
+    field[0, 0:32, 0:TILE] = surf_in[0]
+    field[1, 0:32, 0:TILE] = surf_in[1]
+    field[2, 0:32, 0:TILE] = jnp.sqrt((1.0 + water[1].astype(F32)) / surf_in[2])
+    field[3, 0:32, 0:TILE] = water[0].astype(F32)
+    field[4, 0:32, 0:TILE] = surf_in[3]
+
+    tall = jnp.concatenate([field[f, 0:32, 0:TILE] for f in range(4)], axis=0).T
+    wet = [field[4, 0:32, 0:TILE]] * 3
+    wet = jnp.concatenate(wet + [jnp.zeros((32, TILE), F32)], axis=0).T
+    tall = [tall[ROWS * j : ROWS * (j + 1)] for j in range(nk)]
+    wet = [wet[ROWS * j : ROWS * (j + 1)] for j in range(nk)]
+    wet_down = [pltpu.roll(v, 2, 0) for v in wet]
+    wet_up = [pltpu.roll(v, ROWS - 2, 0) for v in wet]
+    inner = (sub >= 2) & (sub < 6)
+    for j in range(nk):
+        n, m = min(j + 1, nk - 1), max(j - 1, 0)
+        ends = jnp.where(sub < 4, wet_down[n], wet_up[m])
+        mid = jnp.where(lane < 32, wet_down[j], jnp.where(lane < 64, wet_up[j], ends))
+        under_s[j, 0:ROWS, :] = tall[j]
+        under_s[j, ROWS:, :] = jnp.where(inner, mid, jnp.where(sub < 2, tall[n], tall[m]))
+    rim_s[0] = jnp.where(inner, wet_up[nk - 1], tall[nk - 1])
+    rim_s[1] = jnp.where(inner, wet_down[0], tall[0])
+    under_r[k] = under_s[k]
+
+    for c in rest_loads:
+        c.wait()
+    packs = lax.fori_loop(1, nz, first_closures, packs)
+    col_s[0, 0], col_s[0, 1] = packs
+
+    def send_soil(ph):
+        send(row_s.at[ph, 1], row_r.at[ph, 0], f"row{ph}d", down, has_d)
+        send(row_s.at[ph, 0], row_r.at[ph, 1], f"row{ph}u", up, has_u)
+        send(col_s.at[ph, 1], col_r.at[ph, 0], f"col{ph}e", at(0, 1, k), has_e)
+        send(col_s.at[ph, 0], col_r.at[ph, 1], f"col{ph}w", at(0, -1, k), has_w)
+
+    def wait_soil(ph):
+        drain(row_r.at[ph, 0], f"row{ph}d_r", has_u)
+        drain(row_r.at[ph, 1], f"row{ph}u_r", has_d)
+        drain(col_r.at[ph, 0], f"col{ph}e_r", has_w)
+        drain(col_r.at[ph, 1], f"col{ph}w_r", has_e)
+
+    pl.semaphore_wait(barrier, expected)
+    send_soil(0)
+
+    ring(lambda kk: send(under_s.at[kk], under_r.at[k], "under", at(0, 0, kk), keep=False))
+    for dx, ends, has_x, slot in ((1, last, has_e, nk + 1), (-1, first, has_w, nk)):
+
+        @pl.when(ends & has_x)
+        def _():
+            every(
+                lambda kk: send(
+                    under_s.at[kk], under_r.at[slot], f"under{slot}", at(0, dx, kk), keep=False
+                )
+            )
+
+    for i, (dg, has, far) in enumerate(((1, has_s, 0), (-1, has_n, nk - 1))):
+        send(rim_s.at[i], rim_r.at[k], f"rim{i}", at(dg, 0, far), has)
+        for dx, ends, has_x, slot in ((1, last, has_e, nk + 1), (-1, first, has_w, nk)):
+            send(
+                rim_s.at[i], rim_r.at[slot], f"rim{i}{slot}", at(dg, dx, far),
+                has & ends & has_x,
+            )
+
+    def own(a, b):
+        return field.at[:, a:b, 0:TILE]
+
+    send(own(24, 32), own(40, 48), "right", {"grp": g, **right}, has_r)
+    send(own(0, 8), own(32, 40), "left", {"grp": g, **left}, has_l)
+    for dg, has, ref, n in ((1, has_s, above, "s"), (-1, has_n, below, "n")):
+        send(own(0, 32), ref.at[:, 0:32], "line" + n, at(dg, 0, k), has)
+        send(own(24, 32), ref.at[:, 40:48], "right" + n, {"grp": g + dg, **right}, has & has_r)
+        send(own(0, 8), ref.at[:, 32:40], "left" + n, {"grp": g + dg, **left}, has & has_l)
+
     ring(
         lambda kk: send(
             down_s.at[kk], down_r.at[pl.ds(mine, ROWS)], "down", at(0, 0, kk), keep=False
@@ -405,131 +514,6 @@
         send(
             down_s.at[i], edge_r.at[pl.ds(mine, ROWS)], f"edge{dx}", at(0, dx, kk), has_x
         )
-
-    for c in surf_loads + mask_loads:
-        c.wait()
-    field[0, 0:32, 0:TILE] = surf_in[0]
-    field[1, 0:32, 0:TILE] = surf_in[1]
-    field[2, 0:32, 0:TILE] = jnp.sqrt((1.0 + water[1].astype(F32)) / surf_in[2])
-    field[3, 0:32, 0:TILE] = surf_in[3]
-    field[4, 0:32, 0:TILE] = water[0].astype(F32)
-
-    def own(a, b):
-        return field.at[:, a:b, 0:TILE]
-
-    send(own(24, 32), own(40, 48), "right", {"grp": g, **right}, has_r)
-    send(own(0, 8), own(32, 40), "left", {"grp": g, **left}, has_l)
-    for dg, has, ref, n in ((1, has_s, above, "s"), (-1, has_n, below, "n")):
-        send(own(0, 32), ref.at[:, 0:32], "line" + n, at(dg, 0, k), has)
-        send(own(24, 32), ref.at[:, 40:48], "right" + n, {"grp": g + dg, **right}, has & has_r)
-        send(own(0, 8), ref.at[:, 32:40], "left" + n, {"grp": g + dg, **left}, has & has_l)
-
-    for c in rest_loads:
-        c.wait()
-    packs = lax.fori_loop(1, nz, first_closures, packs)
-    col_s[0, 0], col_s[0, 1] = packs
-
-    def send_soil(ph):
-        send(row_s.at[ph, 1], row_r.at[ph, 0], f"row{ph}d", down, has_d)
-        send(row_s.at[ph, 0], row_r.at[ph, 1], f"row{ph}u", up, has_u)
-        send(col_s.at[ph, 1], col_r.at[ph, 0], f"col{ph}e", at(0, 1, k), has_e)
-        send(col_s.at[ph, 0], col_r.at[ph, 1], f"col{ph}w", at(0, -1, k), has_w)
-
-    def wait_soil(ph):
-        drain(row_r.at[ph, 0], f"row{ph}d_r", has_u)
-        drain(row_r.at[ph, 1], f"row{ph}u_r", has_d)
-        drain(col_r.at[ph, 0], f"col{ph}e_r", has_w)
-        drain(col_r.at[ph, 1], f"col{ph}w_r", has_e)
-
-    send_soil(0)
-
-    drain(own(40, 48), "right_r", has_l)
-    drain(own(32, 40), "left_r", has_r)
-    for has, ref, n in ((has_n, above, "s"), (has_s, below, "n")):
-        drain(ref.at[:, 0:32], "line" + n + "_r", has)
-        drain(ref.at[:, 40:48], "right" + n + "_r", has & has_l)
-        drain(ref.at[:, 32:40], "left" + n + "_r", has & has_r)
-    side = lax.broadcasted_iota(jnp.int32, (48, TILE), 1) < 64
-    full = []
-    for f in range(FIELDS):
-        full.append(
-            jnp.concatenate(
-                [field[f, :, 0:TILE], jnp.where(side, below[f], above[f])], axis=1
-            )
-        )
-    w0, level, bed, rain, land = full
-
-    def next_of(v, axis):
-        return pltpu.roll(v, v.shape[axis] - 1, axis)
-
-    def prev_of(v, axis):
-        return pltpu.roll(v, 1, axis)
-
-    faces = [bed * next_of(bed, axis) for axis in (0, 1)]
-
-    def outflow(w):
-        carried = jnp.exp((5.0 / 3.0) * jnp.log(jnp.maximum(w, 1e-30)))
-        surface = level + w
-        total = None
-        for axis in (0, 1):
-            slope = surface - next_of(surface, axis)
-            upwind = jnp.where(slope >= 0, carried, next_of(carried, axis))
-            flux = faces[axis] * upwind * slope * lax.rsqrt(
-                jnp.maximum(jnp.abs(slope), SLOPE_FLOOR)
-            )
-            net = flux - prev_of(flux, axis)
-            total = net if total is None else total + net
-        return total
-
-    out0 = outflow(w0)
-
-    drain(down_s.at[0 : nk - 1], "down_r")
-    drain(down_s.at[0], "down128_r", has_s)
-    drain(down_s.at[0], "down248_r", has_n)
-    for dx, gets in ((1, first & has_w), (-1, last & has_e)):
-        drain(edge_r.at[0:TILE], f"edge{dx}_r", gets)
-        drain(down_s.at[0], f"edge128{dx}_r", gets & has_s)
-        drain(down_s.at[0], f"edge248{dx}_r", gets & has_n)
-
-    tall = lax.broadcasted_iota(jnp.int32, (TILE, TILE), 0)
-    wide_lane = lax.broadcasted_iota(jnp.int32, (TILE, TILE), 1) & 63
-    low = jnp.where(first, 38, 32)
-    use_edge = (wide_lane >= low) & (wide_lane < low + 2) & (first | last)
-
-    def received(a):
-        rows = jnp.where(use_edge, edge_r[a : a + TILE, :], down_r[a : a + TILE, :])
-        if a:
-            rows = jnp.where((tall < ROWS) | (tall >= TILE - ROWS), rows, 0.0)
-        return rows.T
-
-    main, rim = received(0), received(TILE)
-
-    def pick(a):
-        body = [main[a : a + 32], rim[a : a + 32]]
-        halo = [main[a + 32 : a + 40], rim[a + 32 : a + 40]]
-        body, halo = (jnp.concatenate(v, axis=1) for v in (body, halo))
-        return jnp.concatenate([body, halo, halo], axis=0)
-
-    top = pick(0)
-    leak = land * pick(64)
-
-    def advance(w, out):
-        rate = leak * (w - top)
-        return jnp.maximum(w + SURFACE_STEP * (rain - rate - out), 0.0), rate
-
-    w1, rate0 = advance(w0, out0)
-    w2, rate1 = advance(w1, outflow(w1))
-    rate2 = leak * (w2 - top)
-    exchange = SURFACE_STEP * (rate0 + rate1 + rate2)
-    square = jnp.concatenate([exchange[0:32, 0:TILE], jnp.zeros((96, TILE), F32)], axis=0)
-    back_s[...] = square.T.reshape(nk, ROWS, TILE)
-    back_r[k] = back_s[k]
-    ring(
-        lambda kk: send(back_s.at[kk], back_r.at[k], "back", at(0, 0, kk), keep=False)
-    )
-    w3, _ = advance(w2, outflow(w2))
-    surf_in[0] = w3[0:32, 0:TILE]
-    stores = [load(surf_in.at[0], water_out, "water")]
 
     def sums(ph, z, t, halo_rows, halo_cols):
         both = []
@@ -622,26 +606,158 @@
     col_s[1, 0], col_s[1, 1] = packs
     send_soil(1)
 
-    drain(down_s.at[0 : nk - 1], "back_r")
-    extras = []
+    def next_of(v, axis):
+        return pltpu.roll(v, v.shape[axis] - 1, axis)
+
+    def prev_of(v, axis):
+        return pltpu.roll(v, 1, axis)
+
+    def outflow_of(level, bed):
+        faces = [bed * next_of(bed, axis) for axis in (0, 1)]
+
+        def outflow(w):
+            carried = jnp.exp((5.0 / 3.0) * jnp.log(jnp.maximum(w, 1e-30)))
+            surface = level + w
+            total = None
+            for axis in (0, 1):
+                slope = surface - next_of(surface, axis)
+                upwind = jnp.where(slope >= 0, carried, next_of(carried, axis))
+                flux = faces[axis] * upwind * slope * lax.rsqrt(
+                    jnp.maximum(jnp.abs(slope), SLOPE_FLOOR)
+                )
+                net = flux - prev_of(flux, axis)
+                total = net if total is None else total + net
+            return total
+
+        return outflow
+
+    drain(under_s.at[0 : nk - 1], "under_r")
+    drain(under_s.at[0], f"under{nk}_r", has_e)
+    drain(under_s.at[0], f"under{nk + 1}_r", has_w)
+    for i, gets in enumerate((first & has_n, last & has_s)):
+        drain(down_s.at[0:nk], f"rim{i}_r", gets)
+        drain(down_s.at[0], f"rim{i}{nk}_r", gets & has_e)
+        drain(down_s.at[0], f"rim{i}{nk + 1}_r", gets & has_w)
+    use_rim = (first & (sub >= 4) & ((sub >= 6) | (lane >= 64))) | (
+        last & (sub < 4) & ((sub < 2) | (lane >= 64))
+    )
+    near = [under_r[j, 0:ROWS, :] for j in range(nk + 2)]
+    beyond = [jnp.where(use_rim, rim_r[j], under_r[j, ROWS:, :]) for j in range(nk + 2)]
+
+    def gathered(parts, group):
+        out = []
+        for t in range(tiles):
+            v = turn(parts[per * t], -32 * group)
+            for i in range(1, per):
+                v = jnp.where(lane >= 32 * i, turn(parts[per * t + i], 32 * (i - group)), v)
+            out.append(v)
+        ends = turn(parts[nk], -32 * group), turn(parts[nk + 1], 32 * (per - 1 - group))
+        return out + [jnp.where(lane < 64, *ends)]
+
+    def stacked(high, low):
+        high, low = (jnp.concatenate(v, axis=1) for v in (high, low))
+        return jnp.concatenate([high, low], axis=0)
+
+    w, level, bed, land = (stacked(gathered(near, f), gathered(beyond, f)) for f in range(4))
+    parts = [gathered(beyond, f) for f in range(3)]
+
+    def spread(a, b):
+        pairs = zip(a, b)
+        return [
+            jnp.where(sub < 4, pltpu.roll(u, ROWS - 2, 0), pltpu.roll(v, 2, 0)) for u, v in pairs
+        ]
+
+    rain = stacked(spread(parts[0], parts[1]), spread(parts[2], parts[2]))
+    tops = []
+    for i, ref in enumerate((root, flow)):
+        high = [ref[0, 1, :, tile(t)] for t in range(tiles)]
+        low = [
+            jnp.where(sub == 0, row_r[0, 1, i, t, 0:1, :], jnp.where(sub == 7, row_r[0, 0, i, t, 0:1, :], 0.0))
+            for t in range(tiles)
+        ]
+        west, east = (turn(col_r[0, d], v - 64 * i) for d, v in ((0, TILE - 1), (1, 0)))
+        high.append(jnp.where(lane < 64, east, west))
+        tops.append(stacked(high, low + [zero]))
+    q_top, r_top = tops
+    seep = land * q_top * 0.125
+    outflow = outflow_of(level, bed)
+    exchange = None
+    for step in range(3):
+        rate = seep * (q_top * w - r_top)
+        exchange = rate if exchange is None else exchange + rate
+        if step < 2:
+            w = jnp.maximum(w + SURFACE_STEP * (rain - rate - outflow(w)), 0.0)
+    extras = [SURFACE_STEP * exchange[0:ROWS, tile(t)] for t in range(tiles)]
     for t in range(tiles):
-        v = back_r[per * t]
-        for i in range(1, per):
-            v = jnp.where(lane >= 32 * i, turn(back_r[per * t + i], 32 * i), v)
-        source[:, tile(t)] = v
-        extras.append(v)
+        source[:, tile(t)] = extras[t]
     tcol_s[0], tcol_s[1] = second_closures(0, (zero, zero), extras)
     send(top_s.at[1], top_r.at[0], "topd", down, has_d)
     send(top_s.at[0], top_r.at[1], "topu", up, has_u)
     send(tcol_s.at[1], tcol_r.at[0], "tope", at(0, 1, k), has_e)
     send(tcol_s.at[0], tcol_r.at[1], "topw", at(0, -1, k), has_w)
 
+    drain(own(40, 48), "right_r", has_l)
+    drain(own(32, 40), "left_r", has_r)
+    for has, ref, n in ((has_n, above, "s"), (has_s, below, "n")):
+        drain(ref.at[:, 0:32], "line" + n + "_r", has)
+        drain(ref.at[:, 40:48], "right" + n + "_r", has & has_l)
+        drain(ref.at[:, 32:40], "left" + n + "_r", has & has_r)
+    side = lax.broadcasted_iota(jnp.int32, (48, TILE), 1) < 64
+    full = []
+    for f in range(FIELDS):
+        full.append(
+            jnp.concatenate(
+                [field[f, :, 0:TILE], jnp.where(side, below[f], above[f])], axis=1
+            )
+        )
+    w0, level, bed, land, rain = full
+
+    outflow = outflow_of(level, bed)
+    out0 = outflow(w0)
+
+    drain(down_s.at[0 : nk - 1], "down_r")
+    drain(down_s.at[0], "down128_r", has_s)
+    drain(down_s.at[0], "down248_r", has_n)
+    for dx, gets in ((1, first & has_w), (-1, last & has_e)):
+        drain(edge_r.at[0:TILE], f"edge{dx}_r", gets)
+        drain(down_s.at[0], f"edge128{dx}_r", gets & has_s)
+        drain(down_s.at[0], f"edge248{dx}_r", gets & has_n)
+
+    tall = lax.broadcasted_iota(jnp.int32, (TILE, TILE), 0)
+    wide_lane = lax.broadcasted_iota(jnp.int32, (TILE, TILE), 1) & 63
+    low = jnp.where(first, 38, 32)
+    use_edge = (wide_lane >= low) & (wide_lane < low + 2) & (first | last)
+
+    def received(a):
+        rows = jnp.where(use_edge, edge_r[a : a + TILE, :], down_r[a : a + TILE, :])
+        if a:
+            rows = jnp.where((tall < ROWS) | (tall >= TILE - ROWS), rows, 0.0)
+        return rows.T
+
+    main, rim = received(0), received(TILE)
+
+    def pick(a):
+        body = [main[a : a + 32], rim[a : a + 32]]
+        halo = [main[a + 32 : a + 40], rim[a + 32 : a + 40]]
+        body, halo = (jnp.concatenate(v, axis=1) for v in (body, halo))
+        return jnp.concatenate([body, halo, halo], axis=0)
+
+    top = pick(0)
+    leak = land * pick(64)
+
+    def advance(w, out):
+        return jnp.maximum(w + SURFACE_STEP * (rain - leak * (w - top) - out), 0.0)
+
+    for step in range(3):
+        w0 = advance(w0, out0 if step == 0 else outflow(w0))
+    water_out[...] = w0[0:32, 0:TILE]
+
     wait_soil(1)
 
     def last_sweep(z, halo, extra=False):
         for t in range(tiles):
             more = source[:, tile(t)] if extra else None
-            p[z, :, tile(t)] = sweep(
+            head_out[z, :, tile(t)] = sweep(
                 1, z, t, halo, num[z, :, tile(t)], cap[z, :, tile(t)], more
             )
 
@@ -650,16 +766,16 @@
         return carry
 
     lax.fori_loop(1, nz, last_step, 0)
-    stores.append(load(p.at[1:nz], head_out.at[1:nz], "head1"))
     drain(top_r.at[0], "topd_r", has_u)
     drain(top_r.at[1], "topu_r", has_d)
     drain(tcol_r.at[0], "tope_r", has_w)
     drain(tcol_r.at[1], "topw_r", has_e)
     last_sweep(0, top_halo(), True)
-    stores.append(load(p.at[0:1], head_out.at[0:1], "head0"))
 
     drain(down_s.at[0 : nk - 1], "down_s")
-    drain(down_s.at[0 : nk - 1], "back_s")
+    drain(under_s.at[0 : nk - 1], "under_s")
+    drain(under_s, f"under{nk + 1}_s", last & has_e)
+    drain(under_s, f"under{nk}_s", first & has_w)
     drain(down_s.at[0:nk], "down248_s", last & has_s)
     drain(down_s.at[0:nk], "down128_s", first & has_n)
     for copy, when in pending:
@@ -667,8 +783,6 @@
             copy.wait_send()
         else:
             pl.when(when)(copy.wait_send)
-    for c in stores:
-        c.wait()
 
 
 def solution(mesh):
@@ -687,11 +801,11 @@
         head, water = pl.pallas_call(
             functools.partial(kernel, nz, wide, kinds, sizes),
             out_shape=(
-                jax.ShapeDtypeStruct(pressure.shape, F32),
-                jax.ShapeDtypeStruct(depth.shape[::-1], F32),
+                vmem(pressure.shape, F32),
+                vmem(depth.shape[::-1], F32),
             ),
             in_specs=[hbm] * 12,
-            out_specs=(hbm, hbm),
+            out_specs=(pl.BlockSpec(memory_space=vmem),) * 2,
             scratch_shapes=[
                 pltpu.SMEM((4, kinds), F32),
                 vmem(soil, F32),
@@ -717,8 +831,10 @@
                 vmem((nk + 2, ROWS, TILE), F32),
                 vmem((2 * TILE, TILE), F32),
                 vmem((2 * TILE, TILE), F32),
-                vmem((nk, ROWS, TILE), F32),
-                vmem((nk, ROWS, TILE), F32),
+                vmem((nk, 2 * ROWS, TILE), F32),
+                vmem((nk + 2, 2 * ROWS, TILE), F32),
+                vmem((2, ROWS, TILE), F32),
+                vmem((nk + 2, ROWS, TILE), F32),
                 vmem((ROWS, wide), F32),
                 vmem((2, 32, TILE), jnp.int32),
                 pltpu.SemaphoreType.DMA((100,)),

time: 44 us -> 42.2 us (0.959)
  local copies, waits for them, and re-layouts: 2.38 us -> 1.35 us
    unnamed x4 -> x2, local copies, waits for them, and re-layouts: 2.38 us -> 1.35 us
where the time goes in v3:
time: 42.2 us; the launch traced here: 42.1 us
  Pallas kernels  40.1 us (95%)
  local copies, waits for them, and re-layouts  1.35 us (3%)
  between operations  0.64 us (2%)
    pallas_call x1, Pallas kernels, local(): pl.pallas_call(functools.partial(kernel, nz, wide, kinds, sizes), out_sha...  40.1 us
    unnamed x2, local copies, waits for them, and re-layouts  1.35 us

profile of v3, /device:TPU:1, one launch (start us, length us, event | category | flops | bytes accessed | tf_op | source)
XLA Modules:
  0.0 42.1 jit_solution(9092183257154942443)
XLA Ops:
  0.6 40.1 %shard_map.131 = (f32[24,8,512]{2,1,0:T(8,128)S(1)}, f32[32,128]{1,0:T(8,128)S(1)}) custom-call(f32[24,8,512]{2,1,0:T(8,128)} %p_in.1, s32[24,8,512]{2,1,0:T(8,128)} %k_in.1, f32[12]{0:T(128)} %t0_in.1, f32[12]{0:T(128)} %t1_in.1, f32[12]{0:T(128)} %t2_in.1, f32[12]{0:T(128)} %t3_in.1, f32[32,128]{1,0:T(8,128)} %bitcast.8, f32[32,128]{1,0:T(8,128)} %bitcast.9, ...), custom_call_target="tpu_custom_call" | custom-call | tf_op jit(solution)/shard_map/pallas_call | solution.py:801
  40.8 0.7 %copy.16 = f32[24,8,512]{2,1,0:T(8,128)} copy(f32[24,8,512]{2,1,0:T(8,128)S(1)} %get-tuple-element.6) | data formatting | bytes 786432
  41.5 0.6 %copy.17 = f32[128,32]{0,1:T(8,128)} copy(f32[128,32]{0,1:T(8,128)S(1)} %bitcast.7) | data formatting | bytes 32768

commit v4 on v2

--- a/solution.py
+++ b/solution.py
@@ -73,14 +73,14 @@
 
 
 def kernel(
-    nz, wide, kinds, sizes,
+    nz, wide, kinds, sizes, cut_z,
     p_in, k_in, t0_in, t1_in, t2_in, t3_in,
     s0_in, s1_in, s2_in, s3_in, s4_in, s5_in,
     head_out, water_out,
     tab, p, kind, par, cap, sat, root, flow, num,
     row_s, row_r, top_s, top_r, col_s, col_r, tcol_s, tcol_r,
     surf_in, field, below, above,
-    down_s, down_r, edge_r, back_s, back_r, source, water,
+    down_s, down_r, edge_r, back_s, back_r, water,
     sem,
 ):
     ng, nx, nk = sizes
@@ -137,11 +137,8 @@
         pl.semaphore_signal(barrier, 1, device_id=device, device_id_type=MESH)
 
     def ring(body):
-        def step(i, _):
-            body(lax.rem(k + 1 + lax.rem(i + nk // 2 - 1, nk - 1), nk))
-            return 0
-
-        lax.fori_loop(0, nk - 1, step, 0)
+        for away in sorted(range(1, nk), key=lambda d: -min(d, nk - d)):
+            body(jnp.where(k + away >= nk, k + away - nk, k + away))
 
     def every(body):
         def step(i, _):
@@ -258,8 +255,8 @@
 
         @pl.when(jnp.logical_not(has))
         def _():
-            for ph in range(2):
-                col_r[ph, d] = zero
+            for c in range(3):
+                col_r[c, d] = zero
             tcol_r[d] = zero
 
     for d, has in ((0, has_r), (1, has_l)):
@@ -352,8 +349,6 @@
     mine = pl.multiple_of(k * ROWS, ROWS)
     down_r[pl.ds(mine, ROWS), :] = down_s[k]
 
-    pl.semaphore_wait(barrier, expected)
-
     pending = []
 
     def send(src, dst, name, device, when=None, keep=True):
@@ -380,6 +375,20 @@
         else:
             pl.when(when)(wait)
 
+    for c in surf_loads + mask_loads:
+        c.wait()
+    field[0, 0:32, 0:TILE] = surf_in[0]
+    field[1, 0:32, 0:TILE] = surf_in[1]
+    field[2, 0:32, 0:TILE] = jnp.sqrt((1.0 + water[1].astype(F32)) / surf_in[2])
+    field[3, 0:32, 0:TILE] = surf_in[3]
+    field[4, 0:32, 0:TILE] = water[0].astype(F32)
+
+    for c in rest_loads:
+        c.wait()
+    packs = lax.fori_loop(1, nz, first_closures, packs)
+    col_s[0, 0], col_s[0, 1] = packs
+
+    pl.semaphore_wait(barrier, expected)
     ring(
         lambda kk: send(
             down_s.at[kk], down_r.at[pl.ds(mine, ROWS)], "down", at(0, 0, kk), keep=False
@@ -406,13 +415,23 @@
             down_s.at[i], edge_r.at[pl.ds(mine, ROWS)], f"edge{dx}", at(0, dx, kk), has_x
         )
 
-    for c in surf_loads + mask_loads:
-        c.wait()
-    field[0, 0:32, 0:TILE] = surf_in[0]
-    field[1, 0:32, 0:TILE] = surf_in[1]
-    field[2, 0:32, 0:TILE] = jnp.sqrt((1.0 + water[1].astype(F32)) / surf_in[2])
-    field[3, 0:32, 0:TILE] = surf_in[3]
-    field[4, 0:32, 0:TILE] = water[0].astype(F32)
+    chunks = ((0, 0, nz), (1, 0, cut_z), (1, cut_z, nz))
+
+    def send_soil(c):
+        ph, a, b = chunks[c]
+        send(row_s.at[ph, 1, :, :, a:b], row_r.at[ph, 0, :, :, a:b], f"row{c}d", down, has_d)
+        send(row_s.at[ph, 0, :, :, a:b], row_r.at[ph, 1, :, :, a:b], f"row{c}u", up, has_u)
+        send(col_s.at[c, 1], col_r.at[c, 0], f"col{c}e", at(0, 1, k), has_e)
+        send(col_s.at[c, 0], col_r.at[c, 1], f"col{c}w", at(0, -1, k), has_w)
+
+    def wait_soil(c):
+        ph, a, b = chunks[c]
+        drain(row_r.at[ph, 0, :, :, a:b], f"row{c}d_r", has_u)
+        drain(row_r.at[ph, 1, :, :, a:b], f"row{c}u_r", has_d)
+        drain(col_r.at[c, 0], f"col{c}e_r", has_w)
+        drain(col_r.at[c, 1], f"col{c}w_r", has_e)
+
+    send_soil(0)
 
     def own(a, b):
         return field.at[:, a:b, 0:TILE]
@@ -423,113 +442,6 @@
         send(own(0, 32), ref.at[:, 0:32], "line" + n, at(dg, 0, k), has)
         send(own(24, 32), ref.at[:, 40:48], "right" + n, {"grp": g + dg, **right}, has & has_r)
         send(own(0, 8), ref.at[:, 32:40], "left" + n, {"grp": g + dg, **left}, has & has_l)
-
-    for c in rest_loads:
-        c.wait()
-    packs = lax.fori_loop(1, nz, first_closures, packs)
-    col_s[0, 0], col_s[0, 1] = packs
-
-    def send_soil(ph):
-        send(row_s.at[ph, 1], row_r.at[ph, 0], f"row{ph}d", down, has_d)
-        send(row_s.at[ph, 0], row_r.at[ph, 1], f"row{ph}u", up, has_u)
-        send(col_s.at[ph, 1], col_r.at[ph, 0], f"col{ph}e", at(0, 1, k), has_e)
-        send(col_s.at[ph, 0], col_r.at[ph, 1], f"col{ph}w", at(0, -1, k), has_w)
-
-    def wait_soil(ph):
-        drain(row_r.at[ph, 0], f"row{ph}d_r", has_u)
-        drain(row_r.at[ph, 1], f"row{ph}u_r", has_d)
-        drain(col_r.at[ph, 0], f"col{ph}e_r", has_w)
-        drain(col_r.at[ph, 1], f"col{ph}w_r", has_e)
-
-    send_soil(0)
-
-    drain(own(40, 48), "right_r", has_l)
-    drain(own(32, 40), "left_r", has_r)
-    for has, ref, n in ((has_n, above, "s"), (has_s, below, "n")):
-        drain(ref.at[:, 0:32], "line" + n + "_r", has)
-        drain(ref.at[:, 40:48], "right" + n + "_r", has & has_l)
-        drain(ref.at[:, 32:40], "left" + n + "_r", has & has_r)
-    side = lax.broadcasted_iota(jnp.int32, (48, TILE), 1) < 64
-    full = []
-    for f in range(FIELDS):
-        full.append(
-            jnp.concatenate(
-                [field[f, :, 0:TILE], jnp.where(side, below[f], above[f])], axis=1
-            )
-        )
-    w0, level, bed, rain, land = full
-
-    def next_of(v, axis):
-        return pltpu.roll(v, v.shape[axis] - 1, axis)
-
-    def prev_of(v, axis):
-        return pltpu.roll(v, 1, axis)
-
-    faces = [bed * next_of(bed, axis) for axis in (0, 1)]
-
-    def outflow(w):
-        carried = jnp.exp((5.0 / 3.0) * jnp.log(jnp.maximum(w, 1e-30)))
-        surface = level + w
-        total = None
-        for axis in (0, 1):
-            slope = surface - next_of(surface, axis)
-            upwind = jnp.where(slope >= 0, carried, next_of(carried, axis))
-            flux = faces[axis] * upwind * slope * lax.rsqrt(
-                jnp.maximum(jnp.abs(slope), SLOPE_FLOOR)
-            )
-            net = flux - prev_of(flux, axis)
-            total = net if total is None else total + net
-        return total
-
-    out0 = outflow(w0)
-
-    drain(down_s.at[0 : nk - 1], "down_r")
-    drain(down_s.at[0], "down128_r", has_s)
-    drain(down_s.at[0], "down248_r", has_n)
-    for dx, gets in ((1, first & has_w), (-1, last & has_e)):
-        drain(edge_r.at[0:TILE], f"edge{dx}_r", gets)
-        drain(down_s.at[0], f"edge128{dx}_r", gets & has_s)
-        drain(down_s.at[0], f"edge248{dx}_r", gets & has_n)
-
-    tall = lax.broadcasted_iota(jnp.int32, (TILE, TILE), 0)
-    wide_lane = lax.broadcasted_iota(jnp.int32, (TILE, TILE), 1) & 63
-    low = jnp.where(first, 38, 32)
-    use_edge = (wide_lane >= low) & (wide_lane < low + 2) & (first | last)
-
-    def received(a):
-        rows = jnp.where(use_edge, edge_r[a : a + TILE, :], down_r[a : a + TILE, :])
-        if a:
-            rows = jnp.where((tall < ROWS) | (tall >= TILE - ROWS), rows, 0.0)
-        return rows.T
-
-    main, rim = received(0), received(TILE)
-
-    def pick(a):
-        body = [main[a : a + 32], rim[a : a + 32]]
-        halo = [main[a + 32 : a + 40], rim[a + 32 : a + 40]]
-        body, halo = (jnp.concatenate(v, axis=1) for v in (body, halo))
-        return jnp.concatenate([body, halo, halo], axis=0)
-
-    top = pick(0)
-    leak = land * pick(64)
-
-    def advance(w, out):
-        rate = leak * (w - top)
-        return jnp.maximum(w + SURFACE_STEP * (rain - rate - out), 0.0), rate
-
-    w1, rate0 = advance(w0, out0)
-    w2, rate1 = advance(w1, outflow(w1))
-    rate2 = leak * (w2 - top)
-    exchange = SURFACE_STEP * (rate0 + rate1 + rate2)
-    square = jnp.concatenate([exchange[0:32, 0:TILE], jnp.zeros((96, TILE), F32)], axis=0)
-    back_s[...] = square.T.reshape(nk, ROWS, TILE)
-    back_r[k] = back_s[k]
-    ring(
-        lambda kk: send(back_s.at[kk], back_r.at[k], "back", at(0, 0, kk), keep=False)
-    )
-    w3, _ = advance(w2, outflow(w2))
-    surf_in[0] = w3[0:32, 0:TILE]
-    stores = [load(surf_in.at[0], water_out, "water")]
 
     def sums(ph, z, t, halo_rows, halo_cols):
         both = []
@@ -554,63 +466,53 @@
         r += GRAVITY_STEP * (root[ph, z, :, tile(t)] - root[ph, z + 2, :, tile(t)])
         return q, r
 
-    def plain_halo(ph, z):
+    def plain_halo(c, z):
+        ph = chunks[c][0]
+
         def rows(t):
             return [
                 [row_r[ph, d, i, t, pl.ds(z, 1), :] for i in range(2)] for d in range(2)
             ]
 
         cols = [
-            [shift_to(col_r[ph, d], z + 64 * i, (TILE - 1) * d) for i in range(2)]
+            [shift_to(col_r[c, d], z + 64 * i, (TILE - 1) * d) for i in range(2)]
             for d in range(2)
         ]
         return rows, cols
 
-    def top_halo():
-        def rows(t):
-            return [[top_r[d, i : i + 1, tile(t)] for i in range(2)] for d in range(2)]
-
-        cols = [
-            [shift_to(tcol_r[d], 64 * i, (TILE - 1) * d) for i in range(2)]
-            for d in range(2)
-        ]
-        return rows, cols
-
-    def sweep(ph, z, t, halo, base, weight, extra):
+    def sweep_parts(ph, z, t, halo, base, weight):
         rows, cols = halo
         q, r = sums(ph, z, t, rows(t), cols)
         own_root = root[ph, z + 1, :, tile(t)]
-        above_line = base + own_root * r
-        if extra is not None:
-            above_line += extra
-        return above_line / (weight + own_root * q)
-
-    def second_closures(z, packs, extras=None):
+        return base + own_root * r, weight + own_root * q
+
+    def sweep(ph, z, t, halo, base, weight):
+        above_line, below_line = sweep_parts(ph, z, t, halo, base, weight)
+        return above_line / below_line
+
+    def keep(z, t, head, params):
+        c, se, q = closures(head, params)
+        gap = params[4] * (se - sat[z, :, tile(t)])
+        cap[z, :, tile(t)] = c
+        num[z, :, tile(t)] = c * head - gap
+        r = q * head
+        root[1, z + 1, :, tile(t)] = q
+        flow[1, z + 1, :, tile(t)] = r
+        return q, r
+
+    def second_closures(z, packs):
         halo = plain_halo(0, z)
+        heads = []
+        for t in range(tiles):
+            c0 = cap[z, :, tile(t)]
+            heads.append(sweep(0, z, t, halo, c0 * p[z, :, tile(t)], c0))
         ends = []
         for t in range(tiles):
-            c0 = cap[z, :, tile(t)]
-            extra = None if extras is None else extras[t]
-            head = sweep(0, z, t, halo, c0 * p[z, :, tile(t)], c0, extra)
-            params = [par[i, z, :, tile(t)] for i in range(PARAMS)]
-            c, se, q = closures(head, params)
-            r = q * head
-            ends.append((c, se, q, r, head, params[4]))
-        for t in range(tiles):
-            c, se, q, r, head, span = ends[t]
-            gap = span * (se - sat[z, :, tile(t)])
-            cap[z, :, tile(t)] = c
-            num[z, :, tile(t)] = c * head - gap
-            root[1, z + 1, :, tile(t)] = q
-            flow[1, z + 1, :, tile(t)] = r
-            if extras is None:
-                put_row(row_s.at[1, 0], row_s.at[1, 1], 0, z, t, q)
-                put_row(row_s.at[1, 0], row_s.at[1, 1], 1, z, t, r)
-            else:
-                for i, v in ((0, q), (1, r)):
-                    top_s[0, i : i + 1, tile(t)] = v[0:1, :]
-                    top_s[1, i : i + 1, tile(t)] = v[7:8, :]
-        return put_cols(packs, z, *ends[0][2:4], *ends[-1][2:4])
+            q, r = keep(z, t, heads[t], [par[i, z, :, tile(t)] for i in range(PARAMS)])
+            put_row(row_s.at[1, 0], row_s.at[1, 1], 0, z, t, q)
+            put_row(row_s.at[1, 0], row_s.at[1, 1], 1, z, t, r)
+            ends.append((q, r))
+        return put_cols(packs, z, *ends[0], *ends[-1])
 
     for t in range(tiles):
         for d in range(2):
@@ -618,45 +520,189 @@
             for i in range(2):
                 row_s[1, d, i, t, 0:ROWS, :] = zero
     wait_soil(0)
-    packs = lax.fori_loop(1, nz, second_closures, (zero, zero))
-    col_s[1, 0], col_s[1, 1] = packs
-    send_soil(1)
-
-    drain(down_s.at[0 : nk - 1], "back_r")
-    extras = []
+
+    halo = plain_halo(0, 0)
+    west, east = zero, zero
     for t in range(tiles):
-        v = back_r[per * t]
-        for i in range(1, per):
-            v = jnp.where(lane >= 32 * i, turn(back_r[per * t + i], 32 * i), v)
-        source[:, tile(t)] = v
-        extras.append(v)
-    tcol_s[0], tcol_s[1] = second_closures(0, (zero, zero), extras)
+        c0 = cap[0, :, tile(t)]
+        upper, lower = sweep_parts(0, 0, t, halo, c0 * p[0, :, tile(t)], c0)
+        num[0, :, tile(t)] = upper
+        cap[0, :, tile(t)] = lower
+        for i, v in enumerate([upper, lower] + [par[j, 0, :, tile(t)] for j in (0, 1, 2, 5)]):
+            top_s[0, i : i + 1, tile(t)] = v[0:1, :]
+            top_s[1, i : i + 1, tile(t)] = v[ROWS - 1 : ROWS, :]
+            if t == 0:
+                west = jnp.where(lane == i, turn(v, i), west)
+            if t == tiles - 1:
+                east = jnp.where(lane == i, turn(v, i + 1), east)
+    tcol_s[0], tcol_s[1] = west, east
     send(top_s.at[1], top_r.at[0], "topd", down, has_d)
     send(top_s.at[0], top_r.at[1], "topu", up, has_u)
     send(tcol_s.at[1], tcol_r.at[0], "tope", at(0, 1, k), has_e)
     send(tcol_s.at[0], tcol_r.at[1], "topw", at(0, -1, k), has_w)
 
+    packs = lax.fori_loop(1, cut_z, second_closures, (zero, zero))
+    col_s[1, 0], col_s[1, 1] = packs
+    send_soil(1)
+
+    drain(own(40, 48), "right_r", has_l)
+    drain(own(32, 40), "left_r", has_r)
+    for has, ref, n in ((has_n, above, "s"), (has_s, below, "n")):
+        drain(ref.at[:, 0:32], "line" + n + "_r", has)
+        drain(ref.at[:, 40:48], "right" + n + "_r", has & has_l)
+        drain(ref.at[:, 32:40], "left" + n + "_r", has & has_r)
+    side = lax.broadcasted_iota(jnp.int32, (48, TILE), 1) < 64
+    full = []
+    for f in range(FIELDS):
+        full.append(
+            jnp.concatenate(
+                [field[f, :, 0:TILE], jnp.where(side, below[f], above[f])], axis=1
+            )
+        )
+    w0, level, bed, rain, land = full
+
+    def next_of(v, axis):
+        return pltpu.roll(v, v.shape[axis] - 1, axis)
+
+    def prev_of(v, axis):
+        return pltpu.roll(v, 1, axis)
+
+    faces = [bed * next_of(bed, axis) for axis in (0, 1)]
+
+    def outflow(w):
+        carried = jnp.exp((5.0 / 3.0) * jnp.log(jnp.maximum(w, 1e-30)))
+        surface = level + w
+        total = None
+        for axis in (0, 1):
+            slope = surface - next_of(surface, axis)
+            upwind = jnp.where(slope >= 0, carried, next_of(carried, axis))
+            flux = faces[axis] * upwind * slope * lax.rsqrt(
+                jnp.maximum(jnp.abs(slope), SLOPE_FLOOR)
+            )
+            net = flux - prev_of(flux, axis)
+            total = net if total is None else total + net
+        return total
+
+    out0 = outflow(w0)
+
+    drain(down_s.at[0 : nk - 1], "down_r")
+    drain(down_s.at[0], "down128_r", has_s)
+    drain(down_s.at[0], "down248_r", has_n)
+    for dx, gets in ((1, first & has_w), (-1, last & has_e)):
+        drain(edge_r.at[0:TILE], f"edge{dx}_r", gets)
+        drain(down_s.at[0], f"edge128{dx}_r", gets & has_s)
+        drain(down_s.at[0], f"edge248{dx}_r", gets & has_n)
+
+    tall = lax.broadcasted_iota(jnp.int32, (TILE, TILE), 0)
+    wide_lane = lax.broadcasted_iota(jnp.int32, (TILE, TILE), 1) & 63
+    low = jnp.where(first, 38, 32)
+    use_edge = (wide_lane >= low) & (wide_lane < low + 2) & (first | last)
+
+    def received(a):
+        rows = jnp.where(use_edge, edge_r[a : a + TILE, :], down_r[a : a + TILE, :])
+        if a:
+            rows = jnp.where((tall < ROWS) | (tall >= TILE - ROWS), rows, 0.0)
+        return rows.T
+
+    main, rim = received(0), received(TILE)
+
+    def pick(a):
+        body = [main[a : a + 32], rim[a : a + 32]]
+        halo = [main[a + 32 : a + 40], rim[a + 32 : a + 40]]
+        body, halo = (jnp.concatenate(v, axis=1) for v in (body, halo))
+        return jnp.concatenate([body, halo, halo], axis=0)
+
+    top = pick(0)
+    leak = land * pick(64)
+
+    def advance(w, out):
+        rate = leak * (w - top)
+        return jnp.maximum(w + SURFACE_STEP * (rain - rate - out), 0.0), rate
+
+    w1, rate0 = advance(w0, out0)
+    w2, rate1 = advance(w1, outflow(w1))
+    rate2 = leak * (w2 - top)
+    exchange = SURFACE_STEP * (rate0 + rate1 + rate2)
+    body = exchange[0:32]
+    square = jnp.concatenate(
+        [body[:, 0:TILE]] * 2 + [exchange[32:48, 0:TILE], jnp.zeros((48, TILE), F32)], axis=0
+    ).T
+    outer = jnp.concatenate([body[:, TILE:]] * 4, axis=0).T
+    blocks = [square[ROWS * j : ROWS * (j + 1)] for j in range(nk)]
+    blocks = [outer[TILE - ROWS :]] + blocks + [outer[0:ROWS]]
+    second = (lane >= 32) & (lane < 64)
+    for j in range(nk):
+        ends = jnp.where(sub < 4, blocks[j + 2], blocks[j])
+        back_s[j] = jnp.where(second, ends, blocks[j + 1])
+    back_r[k] = back_s[k]
+    ring(
+        lambda kk: send(back_s.at[kk], back_r.at[k], "back", at(0, 0, kk), keep=False)
+    )
+    w3, _ = advance(w2, outflow(w2))
+    water_out[...] = w3[0:32, 0:TILE]
+
+    packs = lax.fori_loop(cut_z, nz, second_closures, (zero, zero))
+    col_s[2, 0], col_s[2, 1] = packs
+    send_soil(2)
+
+    def last_sweep(z, halo):
+        for t in range(tiles):
+            head_out[z, :, tile(t)] = sweep(1, z, t, halo, num[z, :, tile(t)], cap[z, :, tile(t)])
+
+    def last_step(c):
+        def step(z, carry):
+            last_sweep(z, plain_halo(c, z))
+            return carry
+
+        return step
+
     wait_soil(1)
-
-    def last_sweep(z, halo, extra=False):
-        for t in range(tiles):
-            more = source[:, tile(t)] if extra else None
-            p[z, :, tile(t)] = sweep(
-                1, z, t, halo, num[z, :, tile(t)], cap[z, :, tile(t)], more
-            )
-
-    def last_step(z, carry):
-        last_sweep(z, plain_halo(1, z))
-        return carry
-
-    lax.fori_loop(1, nz, last_step, 0)
-    stores.append(load(p.at[1:nz], head_out.at[1:nz], "head1"))
+    lax.fori_loop(2, cut_z - 1, last_step(1), 0)
+    last_sweep(cut_z - 1, plain_halo(1, cut_z - 1))
+    wait_soil(2)
+    lax.fori_loop(cut_z, nz, last_step(2), 0)
     drain(top_r.at[0], "topd_r", has_u)
     drain(top_r.at[1], "topu_r", has_d)
     drain(tcol_r.at[0], "tope_r", has_w)
     drain(tcol_r.at[1], "topw_r", has_e)
-    last_sweep(0, top_halo(), True)
-    stores.append(load(p.at[0:1], head_out.at[0:1], "head0"))
+
+    drain(down_s.at[0 : nk - 1], "back_r")
+
+    def gathered(t, group):
+        v = turn(back_r[per * t], -32 * group)
+        for i in range(1, per):
+            v = jnp.where(lane >= 32 * i, turn(back_r[per * t + i], 32 * (i - group)), v)
+        return v
+
+    def beside(parts, gain):
+        upper, lower, entry, expo, pore, scale = parts
+        head = (upper + gain) / jnp.maximum(lower, 1e-6)
+        _, _, q = closures(head, (entry, expo, pore, 0.0, None, scale))
+        return q, q * head
+
+    extras, rows_beside = [], []
+    for t in range(tiles):
+        extras.append(gathered(t, 0))
+        parts = [
+            jnp.where(sub < 4, top_r[1, i : i + 1, tile(t)], top_r[0, i : i + 1, tile(t)])
+            for i in range(6)
+        ]
+        rows_beside.append(beside(parts, gathered(t, 1)))
+    parts = [
+        jnp.where(lane < 64, turn(tcol_r[0], -i), turn(tcol_r[1], TILE - 1 - i)) for i in range(6)
+    ]
+    gain = jnp.where(lane < 64, turn(back_r[0], TILE - 79), turn(back_r[nk - 1], TILE - 1 - 64))
+    ends = beside(parts, gain)
+    for t in range(tiles):
+        head = (num[0, :, tile(t)] + extras[t]) / cap[0, :, tile(t)]
+        keep(0, t, head, [par[i, 0, :, tile(t)] for i in range(PARAMS)])
+        num[0, :, tile(t)] += extras[t]
+
+    def top_rows(t):
+        return [[v[7:8, :] for v in rows_beside[t]], [v[0:1, :] for v in rows_beside[t]]]
+
+    last_sweep(0, (top_rows, [ends, ends]))
+    last_sweep(1, plain_halo(1, 1))
 
     drain(down_s.at[0 : nk - 1], "down_s")
     drain(down_s.at[0 : nk - 1], "back_s")
@@ -667,8 +713,6 @@
             copy.wait_send()
         else:
             pl.when(when)(copy.wait_send)
-    for c in stores:
-        c.wait()
 
 
 def solution(mesh):
@@ -685,13 +729,13 @@
         soil = (nz, ROWS, wide)
         vmem = pltpu.VMEM
         head, water = pl.pallas_call(
-            functools.partial(kernel, nz, wide, kinds, sizes),
+            functools.partial(kernel, nz, wide, kinds, sizes, 16),
             out_shape=(
-                jax.ShapeDtypeStruct(pressure.shape, F32),
-                jax.ShapeDtypeStruct(depth.shape[::-1], F32),
+                vmem(pressure.shape, F32),
+                vmem(depth.shape[::-1], F32),
             ),
             in_specs=[hbm] * 12,
-            out_specs=(hbm, hbm),
+            out_specs=(pl.BlockSpec(memory_space=vmem),) * 2,
             scratch_shapes=[
                 pltpu.SMEM((4, kinds), F32),
                 vmem(soil, F32),
@@ -706,8 +750,8 @@
                 vmem((2, 2, 2, wide // TILE, nz, TILE), F32),
                 vmem((2, ROWS, wide), F32),
                 vmem((2, ROWS, wide), F32),
-                vmem((2, 2, ROWS, TILE), F32),
-                vmem((2, 2, ROWS, TILE), F32),
+                vmem((3, 2, ROWS, TILE), F32),
+                vmem((3, 2, ROWS, TILE), F32),
                 vmem((2, ROWS, TILE), F32),
                 vmem((2, ROWS, TILE), F32),
                 vmem((4, 32, TILE), F32),
@@ -719,7 +763,6 @@
                 vmem((2 * TILE, TILE), F32),
                 vmem((nk, ROWS, TILE), F32),
                 vmem((nk, ROWS, TILE), F32),
-                vmem((ROWS, wide), F32),
                 vmem((2, 32, TILE), jnp.int32),
                 pltpu.SemaphoreType.DMA((100,)),
             ],

time: 44 us -> 39.8 us (0.905)
  the two profiles are of different devices: /device:TPU:1 before, /device:TPU:24 now
where the time goes in v4:
time: 39.8 us; the launch traced here: 39.6 us
  Pallas kernels  37.6 us (94%)
  local copies, waits for them, and re-layouts  1.35 us (3%)
  between operations  0.64 us (2%)
    pallas_call x1, Pallas kernels, local(): pl.pallas_call(functools.partial(kernel, nz, wide, kinds, sizes, 16), out...  37.6 us
    unnamed x2, local copies, waits for them, and re-layouts  1.35 us

profile of v4, /device:TPU:24, one launch (start us, length us, event | category | flops | bytes accessed | tf_op | source)
XLA Modules:
  0.0 39.6 jit_solution(17816099752333377300)
XLA Ops:
  0.6 37.6 %shard_map.131 = (f32[24,8,512]{2,1,0:T(8,128)S(1)}, f32[32,128]{1,0:T(8,128)S(1)}) custom-call(f32[24,8,512]{2,1,0:T(8,128)} %p_in.1, s32[24,8,512]{2,1,0:T(8,128)} %k_in.1, f32[12]{0:T(128)} %t0_in.1, f32[12]{0:T(128)} %t1_in.1, f32[12]{0:T(128)} %t2_in.1, f32[12]{0:T(128)} %t3_in.1, f32[32,128]{1,0:T(8,128)} %bitcast.8, f32[32,128]{1,0:T(8,128)} %bitcast.9, ...), custom_call_target="tpu_custom_call" | custom-call | tf_op jit(solution)/shard_map/pallas_call | solution.py:731
  38.3 0.7 %copy.16 = f32[24,8,512]{2,1,0:T(8,128)} copy(f32[24,8,512]{2,1,0:T(8,128)S(1)} %get-tuple-element.6) | data formatting | bytes 786432
  39.0 0.6 %copy.17 = f32[128,32]{0,1:T(8,128)} copy(f32[128,32]{0,1:T(8,128)S(1)} %bitcast.7) | data formatting | bytes 32768

commit v5 on v4

--- a/solution.py
+++ b/solution.py
@@ -107,6 +107,73 @@
         copy = pltpu.make_async_copy(src, dst, s(name))
         copy.start()
         return copy
+
+    barrier = pltpu.get_barrier_semaphore()
+
+    def greet(device):
+        pl.semaphore_signal(barrier, 1, device_id=device, device_id_type=MESH)
+
+    def ring(body):
+        for away in sorted(range(1, nk), key=lambda d: -min(d, nk - d)):
+            body(jnp.where(k + away >= nk, k + away - nk, k + away))
+
+    def every(body):
+        def step(i, _):
+            body(i)
+            return 0
+
+        lax.fori_loop(0, nk, step, 0)
+
+    col = x * nk + k
+    has_l, has_r = col > 0, col < nx * nk - 1
+    left = {"gx": jnp.maximum(col - 1, 0) // nk, "gy": lax.rem(jnp.maximum(col - 1, 0), nk)}
+    right = {"gx": (col + 1) // nk, "gy": lax.rem(col + 1, nk)}
+    row = g * nk + k
+    has_u, has_d = row > 0, row < ng * nk - 1
+    up = {"grp": jnp.maximum(row - 1, 0) // nk, "gx": x, "gy": lax.rem(jnp.maximum(row - 1, 0), nk)}
+    down = {"grp": (row + 1) // nk, "gx": x, "gy": lax.rem(row + 1, nk)}
+
+    @pl.when(has_w)
+    def _():
+        @pl.when(first)
+        def _():
+            every(lambda kk: greet(at(0, -1, kk)))
+
+        greet(at(0, -1, k))
+
+    @pl.when(has_e)
+    def _():
+        @pl.when(last)
+        def _():
+            every(lambda kk: greet(at(0, 1, kk)))
+
+        greet(at(0, 1, k))
+
+    for dg, has in ((-1, has_n), (1, has_s)):
+        far = nk - 1 if dg < 0 else 0
+
+        @pl.when(has)
+        def _():
+            greet(at(dg, 0, far))
+            greet(at(dg, 0, k))
+
+            @pl.when(has_l)
+            def _():
+                greet({"grp": g + dg, **left})
+
+            @pl.when(has_r)
+            def _():
+                greet({"grp": g + dg, **right})
+
+            @pl.when(first & has_w)
+            def _():
+                greet(at(dg, -1, far))
+
+            @pl.when(last & has_e)
+            def _():
+                greet(at(dg, 1, far))
+
+    ring(lambda kk: greet(at(0, 0, kk)))
 
     table_loads = [
         load(ref, tab.at[i], f"tab{i}")
@@ -131,72 +198,6 @@
         load(k_in.at[1:nz], kind.at[1:nz], "k1"),
     ]
 
-    barrier = pltpu.get_barrier_semaphore()
-
-    def greet(device):
-        pl.semaphore_signal(barrier, 1, device_id=device, device_id_type=MESH)
-
-    def ring(body):
-        for away in sorted(range(1, nk), key=lambda d: -min(d, nk - d)):
-            body(jnp.where(k + away >= nk, k + away - nk, k + away))
-
-    def every(body):
-        def step(i, _):
-            body(i)
-            return 0
-
-        lax.fori_loop(0, nk, step, 0)
-
-    col = x * nk + k
-    has_l, has_r = col > 0, col < nx * nk - 1
-    left = {"gx": jnp.maximum(col - 1, 0) // nk, "gy": lax.rem(jnp.maximum(col - 1, 0), nk)}
-    right = {"gx": (col + 1) // nk, "gy": lax.rem(col + 1, nk)}
-    row = g * nk + k
-    has_u, has_d = row > 0, row < ng * nk - 1
-    up = {"grp": jnp.maximum(row - 1, 0) // nk, "gx": x, "gy": lax.rem(jnp.maximum(row - 1, 0), nk)}
-    down = {"grp": (row + 1) // nk, "gx": x, "gy": lax.rem(row + 1, nk)}
-
-    ring(lambda kk: greet(at(0, 0, kk)))
-    for dg, has in ((-1, has_n), (1, has_s)):
-        far = nk - 1 if dg < 0 else 0
-
-        @pl.when(has)
-        def _():
-            greet(at(dg, 0, far))
-            greet(at(dg, 0, k))
-
-            @pl.when(has_l)
-            def _():
-                greet({"grp": g + dg, **left})
-
-            @pl.when(has_r)
-            def _():
-                greet({"grp": g + dg, **right})
-
-            @pl.when(first & has_w)
-            def _():
-                greet(at(dg, -1, far))
-
-            @pl.when(last & has_e)
-            def _():
-                greet(at(dg, 1, far))
-
-    @pl.when(has_w)
-    def _():
-        greet(at(0, -1, k))
-
-        @pl.when(first)
-        def _():
-            every(lambda kk: greet(at(0, -1, kk)))
-
-    @pl.when(has_e)
-    def _():
-        greet(at(0, 1, k))
-
-        @pl.when(last)
-        def _():
-            every(lambda kk: greet(at(0, 1, kk)))
-
     def one(flag):
         return flag.astype(jnp.int32)
 
@@ -212,6 +213,8 @@
     )
 
     zero = jnp.zeros((ROWS, TILE), F32)
+    for j in range(nk):
+        back_r[j] = zero
 
     def clear(ref, rows):
         for r in range(0, rows, ROWS):
@@ -389,11 +392,10 @@
     col_s[0, 0], col_s[0, 1] = packs
 
     pl.semaphore_wait(barrier, expected)
-    ring(
-        lambda kk: send(
-            down_s.at[kk], down_r.at[pl.ds(mine, ROWS)], "down", at(0, 0, kk), keep=False
+    for dx, kk, has_x, i in ((1, 0, has_e, nk), (-1, nk - 1, has_w, nk + 1)):
+        send(
+            down_s.at[i], edge_r.at[pl.ds(mine, ROWS)], f"edge{dx}", at(0, dx, kk), has_x
         )
-    )
     for dg, far, has, slot in ((1, last, has_s, 248), (-1, first, has_n, 128)):
 
         @pl.when(far & has)
@@ -410,11 +412,11 @@
                 down_s.at[i], edge_r.at[slot : slot + ROWS], f"edge{slot}{dx}",
                 at(dg, dx, kk), far & has & has_x,
             )
-    for dx, kk, has_x, i in ((1, 0, has_e, nk), (-1, nk - 1, has_w, nk + 1)):
-        send(
-            down_s.at[i], edge_r.at[pl.ds(mine, ROWS)], f"edge{dx}", at(0, dx, kk), has_x
+    ring(
+        lambda kk: send(
+            down_s.at[kk], down_r.at[pl.ds(mine, ROWS)], "down", at(0, 0, kk), keep=False
         )
-
+    )
     chunks = ((0, 0, nz), (1, 0, cut_z), (1, cut_z, nz))
 
     def send_soil(c):
@@ -543,7 +545,6 @@
 
     packs = lax.fori_loop(1, cut_z, second_closures, (zero, zero))
     col_s[1, 0], col_s[1, 1] = packs
-    send_soil(1)
 
     drain(own(40, 48), "right_r", has_l)
     drain(own(32, 40), "left_r", has_r)
@@ -624,20 +625,22 @@
     rate2 = leak * (w2 - top)
     exchange = SURFACE_STEP * (rate0 + rate1 + rate2)
     body = exchange[0:32]
-    square = jnp.concatenate(
-        [body[:, 0:TILE]] * 2 + [exchange[32:48, 0:TILE], jnp.zeros((48, TILE), F32)], axis=0
-    ).T
+    mesh_t = [body[:, 0:TILE]] * 3 + [exchange[32:48, 0:TILE]] * 2
+    square = jnp.concatenate(mesh_t, axis=0).T
     outer = jnp.concatenate([body[:, TILE:]] * 4, axis=0).T
     blocks = [square[ROWS * j : ROWS * (j + 1)] for j in range(nk)]
     blocks = [outer[TILE - ROWS :]] + blocks + [outer[0:ROWS]]
-    second = (lane >= 32) & (lane < 64)
+    folded = [pltpu.roll(v, 4, 0) for v in blocks]
+    fold = ((lane >= 32) & (lane < 64)) | (lane >= 112)
+    rim = (lane >= 64) & (lane < 96)
     for j in range(nk):
-        ends = jnp.where(sub < 4, blocks[j + 2], blocks[j])
-        back_s[j] = jnp.where(second, ends, blocks[j + 1])
+        ends = jnp.where(sub < 2, blocks[j + 2], folded[j])
+        back_s[j] = jnp.where(rim, ends, jnp.where(fold, folded[j + 1], blocks[j + 1]))
     back_r[k] = back_s[k]
     ring(
-        lambda kk: send(back_s.at[kk], back_r.at[k], "back", at(0, 0, kk), keep=False)
+        lambda kk: send(back_s.at[kk, 0:4], back_r.at[k, 0:4], "back", at(0, 0, kk), keep=False)
     )
+    send_soil(1)
     w3, _ = advance(w2, outflow(w2))
     water_out[...] = w3[0:32, 0:TILE]
 
@@ -666,7 +669,7 @@
     drain(tcol_r.at[0], "tope_r", has_w)
     drain(tcol_r.at[1], "topw_r", has_e)
 
-    drain(down_s.at[0 : nk - 1], "back_r")
+    drain(down_s.at[0 : nk - 1, 0:4], "back_r")
 
     def gathered(t, group):
         v = turn(back_r[per * t], -32 * group)
@@ -674,6 +677,9 @@
             v = jnp.where(lane >= 32 * i, turn(back_r[per * t + i], 32 * (i - group)), v)
         return v
 
+    def unfold(a, b):
+        return jnp.where(sub < 4, a, pltpu.roll(b, 4, 0))
+
     def beside(parts, gain):
         upper, lower, entry, expo, pore, scale = parts
         head = (upper + gain) / jnp.maximum(lower, 1e-6)
@@ -682,16 +688,20 @@
 
     extras, rows_beside = [], []
     for t in range(tiles):
-        extras.append(gathered(t, 0))
+        extras.append(unfold(gathered(t, 0), gathered(t, 1)))
         parts = [
-            jnp.where(sub < 4, top_r[1, i : i + 1, tile(t)], top_r[0, i : i + 1, tile(t)])
+            jnp.where(sub < 2, top_r[1, i : i + 1, tile(t)], top_r[0, i : i + 1, tile(t)])
             for i in range(6)
         ]
-        rows_beside.append(beside(parts, gathered(t, 1)))
+        rows_beside.append(beside(parts, gathered(t, 2)))
     parts = [
         jnp.where(lane < 64, turn(tcol_r[0], -i), turn(tcol_r[1], TILE - 1 - i)) for i in range(6)
     ]
-    gain = jnp.where(lane < 64, turn(back_r[0], TILE - 79), turn(back_r[nk - 1], TILE - 1 - 64))
+    west, east = back_r[0], back_r[nk - 1]
+    gain = unfold(
+        jnp.where(lane < 64, turn(west, -111), turn(east, 31)),
+        jnp.where(lane < 64, turn(west, -127), turn(east, 15)),
+    )
     ends = beside(parts, gain)
     for t in range(tiles):
         head = (num[0, :, tile(t)] + extras[t]) / cap[0, :, tile(t)]
@@ -699,13 +709,13 @@
         num[0, :, tile(t)] += extras[t]
 
     def top_rows(t):
-        return [[v[7:8, :] for v in rows_beside[t]], [v[0:1, :] for v in rows_beside[t]]]
+        return [[v[3:4, :] for v in rows_beside[t]], [v[0:1, :] for v in rows_beside[t]]]
 
     last_sweep(0, (top_rows, [ends, ends]))
     last_sweep(1, plain_halo(1, 1))
 
     drain(down_s.at[0 : nk - 1], "down_s")
-    drain(down_s.at[0 : nk - 1], "back_s")
+    drain(down_s.at[0 : nk - 1, 0:4], "back_s")
     drain(down_s.at[0:nk], "down248_s", last & has_s)
     drain(down_s.at[0:nk], "down128_s", first & has_n)
     for copy, when in pending:

time: 39.8 us -> 38.5 us (0.967)
  the two profiles are of different devices: /device:TPU:24 before, /device:TPU:1 now
where the time goes in v5:
time: 38.5 us; the launch traced here: 38.4 us
  Pallas kernels  36.4 us (95%)
  local copies, waits for them, and re-layouts  1.35 us (4%)
  between operations  0.64 us (2%)
    pallas_call x1, Pallas kernels, local(): pl.pallas_call(functools.partial(kernel, nz, wide, kinds, sizes, 16), out...  36.4 us
    unnamed x2, local copies, waits for them, and re-layouts  1.35 us

profile of v5, /device:TPU:1, one launch (start us, length us, event | category | flops | bytes accessed | tf_op | source)
XLA Modules:
  0.0 38.4 jit_solution(13709319528990117821)
XLA Ops:
  0.6 36.4 %shard_map.131 = (f32[24,8,512]{2,1,0:T(8,128)S(1)}, f32[32,128]{1,0:T(8,128)S(1)}) custom-call(f32[24,8,512]{2,1,0:T(8,128)} %p_in.1, s32[24,8,512]{2,1,0:T(8,128)} %k_in.1, f32[12]{0:T(128)} %t0_in.1, f32[12]{0:T(128)} %t1_in.1, f32[12]{0:T(128)} %t2_in.1, f32[12]{0:T(128)} %t3_in.1, f32[32,128]{1,0:T(8,128)} %bitcast.8, f32[32,128]{1,0:T(8,128)} %bitcast.9, ...), custom_call_target="tpu_custom_call" | custom-call | tf_op jit(solution)/shard_map/pallas_call | solution.py:741
  37.0 0.7 %copy.16 = f32[24,8,512]{2,1,0:T(8,128)} copy(f32[24,8,512]{2,1,0:T(8,128)S(1)} %get-tuple-element.6) | data formatting | bytes 786432
  37.8 0.6 %copy.17 = f32[128,32]{0,1:T(8,128)} copy(f32[128,32]{0,1:T(8,128)S(1)} %bitcast.7) | data formatting | bytes 32768

commit v6 on v5

--- a/solution.py
+++ b/solution.py
@@ -388,7 +388,7 @@
 
     for c in rest_loads:
         c.wait()
-    packs = lax.fori_loop(1, nz, first_closures, packs)
+    packs = lax.fori_loop(1, nz, first_closures, packs, unroll=4)
     col_s[0, 0], col_s[0, 1] = packs
 
     pl.semaphore_wait(barrier, expected)
@@ -445,28 +445,28 @@
         send(own(24, 32), ref.at[:, 40:48], "right" + n, {"grp": g + dg, **right}, has & has_r)
         send(own(0, 8), ref.at[:, 32:40], "left" + n, {"grp": g + dg, **left}, has & has_l)
 
-    def sums(ph, z, t, halo_rows, halo_cols):
+    def sums(ph, z, halo):
+        rows, cols = halo
         both = []
         for i, ref in enumerate((root, flow)):
-            mid = ref[ph, z + 1, :, tile(t)]
-            total = ref[ph, z, :, tile(t)] + ref[ph, z + 2, :, tile(t)]
-            above_row, below_row = halo_rows[0][i], halo_rows[1][i]
-            total += jnp.where(sub == 0, above_row, pltpu.roll(mid, 1, 0))
-            total += jnp.where(sub == ROWS - 1, below_row, pltpu.roll(mid, ROWS - 1, 0))
-            if t > 0:
-                west = pltpu.roll(ref[ph, z + 1, :, tile(t - 1)], 1, 1)
-            else:
-                west = halo_cols[0][i]
-            if t + 1 < tiles:
-                east = pltpu.roll(ref[ph, z + 1, :, tile(t + 1)], TILE - 1, 1)
-            else:
-                east = halo_cols[1][i]
-            total += jnp.where(lane == 0, west, pltpu.roll(mid, 1, 1))
-            total += jnp.where(lane == TILE - 1, east, pltpu.roll(mid, TILE - 1, 1))
-            both.append(total)
-        q, r = both
-        r += GRAVITY_STEP * (root[ph, z, :, tile(t)] - root[ph, z + 2, :, tile(t)])
-        return q, r
+            mid = [ref[ph, z + 1, :, tile(t)] for t in range(tiles)]
+            from_west = [cols[0][i]] + [pltpu.roll(v, 1, 1) for v in mid]
+            from_east = [pltpu.roll(v, TILE - 1, 1) for v in mid] + [cols[1][i]]
+            totals = []
+            for t in range(tiles):
+                high, low = ref[ph, z, :, tile(t)], ref[ph, z + 2, :, tile(t)]
+                ends = rows(t)
+                north = jnp.where(sub == 0, ends[0][i], pltpu.roll(mid[t], 1, 0))
+                south = jnp.where(sub == ROWS - 1, ends[1][i], pltpu.roll(mid[t], ROWS - 1, 0))
+                west = jnp.where(lane == 0, from_west[t], from_west[t + 1])
+                east = jnp.where(lane == TILE - 1, from_east[t + 1], from_east[t])
+                totals.append(((high + low) + (north + south)) + (west + east))
+                if i == 0:
+                    both.append(GRAVITY_STEP * (high - low))
+            both.append((mid, totals))
+        own_root, q = both[tiles]
+        r = both[tiles + 1][1]
+        return own_root, q, [r[t] + both[t] for t in range(tiles)]
 
     def plain_halo(c, z):
         ph = chunks[c][0]
@@ -482,15 +482,16 @@
         ]
         return rows, cols
 
-    def sweep_parts(ph, z, t, halo, base, weight):
-        rows, cols = halo
-        q, r = sums(ph, z, t, rows(t), cols)
-        own_root = root[ph, z + 1, :, tile(t)]
-        return base + own_root * r, weight + own_root * q
-
-    def sweep(ph, z, t, halo, base, weight):
-        above_line, below_line = sweep_parts(ph, z, t, halo, base, weight)
-        return above_line / below_line
+    def sweep_parts(ph, z, halo, base, weight):
+        own_root, q, r = sums(ph, z, halo)
+        return [
+            (base[t] + own_root[t] * r[t], weight[t] + own_root[t] * q[t]) for t in range(tiles)
+        ]
+
+    def first_parts(z, halo):
+        weight = [cap[z, :, tile(t)] for t in range(tiles)]
+        base = [weight[t] * p[z, :, tile(t)] for t in range(tiles)]
+        return sweep_parts(0, z, halo, base, weight)
 
     def keep(z, t, head, params):
         c, se, q = closures(head, params)
@@ -504,10 +505,7 @@
 
     def second_closures(z, packs):
         halo = plain_halo(0, z)
-        heads = []
-        for t in range(tiles):
-            c0 = cap[z, :, tile(t)]
-            heads.append(sweep(0, z, t, halo, c0 * p[z, :, tile(t)], c0))
+        heads = [upper / lower for upper, lower in first_parts(z, halo)]
         ends = []
         for t in range(tiles):
             q, r = keep(z, t, heads[t], [par[i, z, :, tile(t)] for i in range(PARAMS)])
@@ -525,9 +523,7 @@
 
     halo = plain_halo(0, 0)
     west, east = zero, zero
-    for t in range(tiles):
-        c0 = cap[0, :, tile(t)]
-        upper, lower = sweep_parts(0, 0, t, halo, c0 * p[0, :, tile(t)], c0)
+    for t, (upper, lower) in enumerate(first_parts(0, halo)):
         num[0, :, tile(t)] = upper
         cap[0, :, tile(t)] = lower
         for i, v in enumerate([upper, lower] + [par[j, 0, :, tile(t)] for j in (0, 1, 2, 5)]):
@@ -543,7 +539,7 @@
     send(tcol_s.at[1], tcol_r.at[0], "tope", at(0, 1, k), has_e)
     send(tcol_s.at[0], tcol_r.at[1], "topw", at(0, -1, k), has_w)
 
-    packs = lax.fori_loop(1, cut_z, second_closures, (zero, zero))
+    packs = lax.fori_loop(1, cut_z, second_closures, (zero, zero), unroll=4)
     col_s[1, 0], col_s[1, 1] = packs
 
     drain(own(40, 48), "right_r", has_l)
@@ -644,13 +640,15 @@
     w3, _ = advance(w2, outflow(w2))
     water_out[...] = w3[0:32, 0:TILE]
 
-    packs = lax.fori_loop(cut_z, nz, second_closures, (zero, zero))
+    packs = lax.fori_loop(cut_z, nz, second_closures, (zero, zero), unroll=4)
     col_s[2, 0], col_s[2, 1] = packs
     send_soil(2)
 
     def last_sweep(z, halo):
-        for t in range(tiles):
-            head_out[z, :, tile(t)] = sweep(1, z, t, halo, num[z, :, tile(t)], cap[z, :, tile(t)])
+        base = [num[z, :, tile(t)] for t in range(tiles)]
+        weight = [cap[z, :, tile(t)] for t in range(tiles)]
+        for t, (upper, lower) in enumerate(sweep_parts(1, z, halo, base, weight)):
+            head_out[z, :, tile(t)] = upper / lower
 
     def last_step(c):
         def step(z, carry):
@@ -660,10 +658,10 @@
         return step
 
     wait_soil(1)
-    lax.fori_loop(2, cut_z - 1, last_step(1), 0)
+    lax.fori_loop(2, cut_z - 1, last_step(1), 0, unroll=4)
     last_sweep(cut_z - 1, plain_halo(1, cut_z - 1))
     wait_soil(2)
-    lax.fori_loop(cut_z, nz, last_step(2), 0)
+    lax.fori_loop(cut_z, nz, last_step(2), 0, unroll=4)
     drain(top_r.at[0], "topd_r", has_u)
     drain(top_r.at[1], "topu_r", has_d)
     drain(tcol_r.at[0], "tope_r", has_w)

time: 38.5 us -> 36.3 us (0.943); the launches traced: 38.4 us -> 35.7 us
  Pallas kernels: 36.4 us -> 33.7 us
    pallas_call x1, Pallas kernels: 36.4 us -> 33.7 us  [local(): pl.pallas_call(functools.partial(kernel, nz, wide, kinds, sizes, 16), out...]
where the time goes in v6:
time: 36.3 us; the launch traced here: 35.7 us
  Pallas kernels  33.7 us (93%)
  local copies, waits for them, and re-layouts  1.35 us (4%)
  between operations  0.64 us (2%)
    pallas_call x1, Pallas kernels, local(): pl.pallas_call(functools.partial(kernel, nz, wide, kinds, sizes, 16), out...  33.7 us
    unnamed x2, local copies, waits for them, and re-layouts  1.35 us

profile of v6, /device:TPU:1, one launch (start us, length us, event | category | flops | bytes accessed | tf_op | source)
XLA Modules:
  0.0 35.7 jit_solution(14295257338855323768)
XLA Ops:
  0.6 33.7 %shard_map.131 = (f32[24,8,512]{2,1,0:T(8,128)S(1)}, f32[32,128]{1,0:T(8,128)S(1)}) custom-call(f32[24,8,512]{2,1,0:T(8,128)} %p_in.1, s32[24,8,512]{2,1,0:T(8,128)} %k_in.1, f32[12]{0:T(128)} %t0_in.1, f32[12]{0:T(128)} %t1_in.1, f32[12]{0:T(128)} %t2_in.1, f32[12]{0:T(128)} %t3_in.1, f32[32,128]{1,0:T(8,128)} %bitcast.8, f32[32,128]{1,0:T(8,128)} %bitcast.9, ...), custom_call_target="tpu_custom_call" | custom-call | tf_op jit(solution)/shard_map/pallas_call | solution.py:739
  34.3 0.7 %copy.16 = f32[24,8,512]{2,1,0:T(8,128)} copy(f32[24,8,512]{2,1,0:T(8,128)S(1)} %get-tuple-element.6) | data formatting | bytes 786432
  35.0 0.6 %copy.17 = f32[128,32]{0,1:T(8,128)} copy(f32[128,32]{0,1:T(8,128)S(1)} %bitcast.7) | data formatting | bytes 32768

commit v7 on v6

--- a/solution.py
+++ b/solution.py
@@ -667,6 +667,16 @@
     drain(tcol_r.at[0], "tope_r", has_w)
     drain(tcol_r.at[1], "topw_r", has_e)
 
+    drain(down_s.at[0 : nk - 1], "down_s")
+    drain(down_s.at[0 : nk - 1, 0:4], "back_s")
+    drain(down_s.at[0:nk], "down248_s", last & has_s)
+    drain(down_s.at[0:nk], "down128_s", first & has_n)
+    for copy, when in pending:
+        if when is None:
+            copy.wait_send()
+        else:
+            pl.when(when)(copy.wait_send)
+
     drain(down_s.at[0 : nk - 1, 0:4], "back_r")
 
     def gathered(t, group):
@@ -712,15 +722,16 @@
     last_sweep(0, (top_rows, [ends, ends]))
     last_sweep(1, plain_halo(1, 1))
 
-    drain(down_s.at[0 : nk - 1], "down_s")
-    drain(down_s.at[0 : nk - 1, 0:4], "back_s")
-    drain(down_s.at[0:nk], "down248_s", last & has_s)
-    drain(down_s.at[0:nk], "down128_s", first & has_n)
-    for copy, when in pending:
-        if when is None:
-            copy.wait_send()
-        else:
-            pl.when(when)(copy.wait_send)
+
+def deliver(head, water, head_out, water_out, sem):
+    copies = [
+        pltpu.make_async_copy(head, head_out, sem.at[0]),
+        pltpu.make_async_copy(water, water_out, sem.at[1]),
+    ]
+    for c in copies:
+        c.start()
+    for c in copies:
+        c.wait()
 
 
 def solution(mesh):
@@ -781,6 +792,17 @@
             pressure, soil_class, capacity_range, inverse_entry, shape_index, conductivity,
             depth.T, elevation.T, roughness.T, rain.T, land_mask.T, channel_mask.T,
         )
+        head, water = pl.pallas_call(
+            deliver,
+            out_shape=(
+                pltpu.HBM(head.shape, F32),
+                pltpu.HBM(water.shape, F32),
+            ),
+            in_specs=[pl.BlockSpec(memory_space=vmem)] * 2,
+            out_specs=(hbm, hbm),
+            scratch_shapes=[pltpu.SemaphoreType.DMA((2,))],
+            compiler_params=pltpu.CompilerParams(vmem_limit_bytes=2 * 1024 * 1024),
+        )(head, water)
         return head, water.T
 
     tile = P(None, ("grp", "gy"), "gx")

time: 36.3 us -> 35.7 us (0.983)
  local copies, waits for them, and re-layouts: 1.35 us -> 0 us
  Pallas kernels: 33.7 us -> 34.4 us
    unnamed x2 -> x0, local copies, waits for them, and re-layouts: 1.35 us -> none
    pallas_call x0 -> x1, Pallas kernels: none -> 0.77 us  [local(): pl.pallas_call(deliver, out_shape=(pltpu.HBM(head.shape, F32), pltpu.HBM(...]
where the time goes in v7:
time: 35.7 us; the launch traced here: 35.1 us
  Pallas kernels  34.4 us (96%)
  between operations  0.64 us (2%)
    pallas_call x1, Pallas kernels, local(): pl.pallas_call(functools.partial(kernel, nz, wide, kinds, sizes, 16), out...  33.7 us
    pallas_call x1, Pallas kernels, local(): pl.pallas_call(deliver, out_shape=(pltpu.HBM(head.shape, F32), pltpu.HBM(...  0.77 us

profile of v7, /device:TPU:1, one launch (start us, length us, event | category | flops | bytes accessed | tf_op | source)
XLA Modules:
  0.0 35.1 jit_solution(14434563333498080690)
XLA Ops:
  0.6 33.7 %shard_map.131 = (f32[24,8,512]{2,1,0:T(8,128)S(1)}, f32[32,128]{1,0:T(8,128)S(1)}) custom-call(f32[24,8,512]{2,1,0:T(8,128)} %p_in.1, s32[24,8,512]{2,1,0:T(8,128)} %k_in.1, f32[12]{0:T(128)} %t0_in.1, f32[12]{0:T(128)} %t1_in.1, f32[12]{0:T(128)} %t2_in.1, f32[12]{0:T(128)} %t3_in.1, f32[32,128]{1,0:T(8,128)} %bitcast.7, f32[32,128]{1,0:T(8,128)} %bitcast.8, ...), custom_call_target="tpu_custom_call" | custom-call | tf_op jit(solution)/shard_map/pallas_call | solution.py:750
  34.3 0.8 %shard_map.132 = (f32[24,8,512]{2,1,0:T(8,128)}, f32[32,128]{1,0:T(8,128)}) custom-call(f32[24,8,512]{2,1,0:T(8,128)S(1)} %get-tuple-element.6.head, f32[32,128]{1,0:T(8,128)S(1)} %get-tuple-element.7.water), custom_call_target="tpu_custom_call" | custom-call | tf_op jit(solution)/shard_map/pallas_call | solution.py:795

commit v8 on v7

--- a/solution.py
+++ b/solution.py
@@ -748,7 +748,7 @@
         soil = (nz, ROWS, wide)
         vmem = pltpu.VMEM
         head, water = pl.pallas_call(
-            functools.partial(kernel, nz, wide, kinds, sizes, 16),
+            functools.partial(kernel, nz, wide, kinds, sizes, 8),
             out_shape=(
                 vmem(pressure.shape, F32),
                 vmem(depth.shape[::-1], F32),

time: 35.7 us -> 35.8 us (level); the launches traced: 35.1 us -> 35.6 us
  Pallas kernels: 34.4 us -> 35 us
    pallas_call x1, Pallas kernels: 33.7 us -> 34.2 us  [local(): pl.pallas_call(functools.partial(kernel, nz, wide, kinds, sizes, 8), out_...]
where the time goes in v8:
time: 35.8 us; the launch traced here: 35.6 us
  Pallas kernels  35 us (98%)
  between operations  0.64 us (2%)
    pallas_call x1, Pallas kernels, local(): pl.pallas_call(functools.partial(kernel, nz, wide, kinds, sizes, 8), out_...  34.2 us
    pallas_call x1, Pallas kernels, local(): pl.pallas_call(deliver, out_shape=(pltpu.HBM(head.shape, F32), pltpu.HBM(...  0.77 us

profile of v8, /device:TPU:1, one launch (start us, length us, event | category | flops | bytes accessed | tf_op | source)
XLA Modules:
  0.0 35.6 jit_solution(8157324469897964256)
XLA Ops:
  0.6 34.2 %shard_map.131 = (f32[24,8,512]{2,1,0:T(8,128)S(1)}, f32[32,128]{1,0:T(8,128)S(1)}) custom-call(f32[24,8,512]{2,1,0:T(8,128)} %p_in.1, s32[24,8,512]{2,1,0:T(8,128)} %k_in.1, f32[12]{0:T(128)} %t0_in.1, f32[12]{0:T(128)} %t1_in.1, f32[12]{0:T(128)} %t2_in.1, f32[12]{0:T(128)} %t3_in.1, f32[32,128]{1,0:T(8,128)} %bitcast.7, f32[32,128]{1,0:T(8,128)} %bitcast.8, ...), custom_call_target="tpu_custom_call" | custom-call | tf_op jit(solution)/shard_map/pallas_call | solution.py:750
  34.8 0.8 %shard_map.132 = (f32[24,8,512]{2,1,0:T(8,128)}, f32[32,128]{1,0:T(8,128)}) custom-call(f32[24,8,512]{2,1,0:T(8,128)S(1)} %get-tuple-element.6.head, f32[32,128]{1,0:T(8,128)S(1)} %get-tuple-element.7.water), custom_call_target="tpu_custom_call" | custom-call | tf_op jit(solution)/shard_map/pallas_call | solution.py:795

commit v9 on v7

--- a/solution.py
+++ b/solution.py
@@ -392,6 +392,24 @@
     col_s[0, 0], col_s[0, 1] = packs
 
     pl.semaphore_wait(barrier, expected)
+    chunks = ((0, 0, nz), (1, 0, cut_z), (1, cut_z, nz))
+
+    def send_soil(c):
+        ph, a, b = chunks[c]
+        send(row_s.at[ph, 1, :, :, a:b], row_r.at[ph, 0, :, :, a:b], f"row{c}d", down, has_d)
+        send(row_s.at[ph, 0, :, :, a:b], row_r.at[ph, 1, :, :, a:b], f"row{c}u", up, has_u)
+        send(col_s.at[c, 1], col_r.at[c, 0], f"col{c}e", at(0, 1, k), has_e)
+        send(col_s.at[c, 0], col_r.at[c, 1], f"col{c}w", at(0, -1, k), has_w)
+
+    def wait_soil(c):
+        ph, a, b = chunks[c]
+        drain(row_r.at[ph, 0, :, :, a:b], f"row{c}d_r", has_u)
+        drain(row_r.at[ph, 1, :, :, a:b], f"row{c}u_r", has_d)
+        drain(col_r.at[c, 0], f"col{c}e_r", has_w)
+        drain(col_r.at[c, 1], f"col{c}w_r", has_e)
+
+    send_soil(0)
+
     for dx, kk, has_x, i in ((1, 0, has_e, nk), (-1, nk - 1, has_w, nk + 1)):
         send(
             down_s.at[i], edge_r.at[pl.ds(mine, ROWS)], f"edge{dx}", at(0, dx, kk), has_x
@@ -417,23 +435,6 @@
             down_s.at[kk], down_r.at[pl.ds(mine, ROWS)], "down", at(0, 0, kk), keep=False
         )
     )
-    chunks = ((0, 0, nz), (1, 0, cut_z), (1, cut_z, nz))
-
-    def send_soil(c):
-        ph, a, b = chunks[c]
-        send(row_s.at[ph, 1, :, :, a:b], row_r.at[ph, 0, :, :, a:b], f"row{c}d", down, has_d)
-        send(row_s.at[ph, 0, :, :, a:b], row_r.at[ph, 1, :, :, a:b], f"row{c}u", up, has_u)
-        send(col_s.at[c, 1], col_r.at[c, 0], f"col{c}e", at(0, 1, k), has_e)
-        send(col_s.at[c, 0], col_r.at[c, 1], f"col{c}w", at(0, -1, k), has_w)
-
-    def wait_soil(c):
-        ph, a, b = chunks[c]
-        drain(row_r.at[ph, 0, :, :, a:b], f"row{c}d_r", has_u)
-        drain(row_r.at[ph, 1, :, :, a:b], f"row{c}u_r", has_d)
-        drain(col_r.at[c, 0], f"col{c}e_r", has_w)
-        drain(col_r.at[c, 1], f"col{c}w_r", has_e)
-
-    send_soil(0)
 
     def own(a, b):
         return field.at[:, a:b, 0:TILE]

time: 35.7 us -> 37.2 us (1.042); the launches traced: 35.1 us -> 37.1 us
  Pallas kernels: 34.4 us -> 36.5 us
    pallas_call x1, Pallas kernels: 33.7 us -> 35.7 us  [local(): pl.pallas_call(functools.partial(kernel, nz, wide, kinds, sizes, 16), out...]
where the time goes in v9:
time: 37.2 us; the launch traced here: 37.1 us
  Pallas kernels  36.5 us (98%)
  between operations  0.64 us (2%)
    pallas_call x1, Pallas kernels, local(): pl.pallas_call(functools.partial(kernel, nz, wide, kinds, sizes, 16), out...  35.7 us
    pallas_call x1, Pallas kernels, local(): pl.pallas_call(deliver, out_shape=(pltpu.HBM(head.shape, F32), pltpu.HBM(...  0.77 us

profile of v9, /device:TPU:1, one launch (start us, length us, event | category | flops | bytes accessed | tf_op | source)
XLA Modules:
  0.0 37.1 jit_solution(10333912588540230065)
XLA Ops:
  0.6 35.7 %shard_map.131 = (f32[24,8,512]{2,1,0:T(8,128)S(1)}, f32[32,128]{1,0:T(8,128)S(1)}) custom-call(f32[24,8,512]{2,1,0:T(8,128)} %p_in.1, s32[24,8,512]{2,1,0:T(8,128)} %k_in.1, f32[12]{0:T(128)} %t0_in.1, f32[12]{0:T(128)} %t1_in.1, f32[12]{0:T(128)} %t2_in.1, f32[12]{0:T(128)} %t3_in.1, f32[32,128]{1,0:T(8,128)} %bitcast.7, f32[32,128]{1,0:T(8,128)} %bitcast.8, ...), custom_call_target="tpu_custom_call" | custom-call | tf_op jit(solution)/shard_map/pallas_call | solution.py:751
  36.3 0.8 %shard_map.132 = (f32[24,8,512]{2,1,0:T(8,128)}, f32[32,128]{1,0:T(8,128)}) custom-call(f32[24,8,512]{2,1,0:T(8,128)S(1)} %get-tuple-element.6.head, f32[32,128]{1,0:T(8,128)S(1)} %get-tuple-element.7.water), custom_call_target="tpu_custom_call" | custom-call | tf_op jit(solution)/shard_map/pallas_call | solution.py:796

commit v10 on v7

--- a/solution.py
+++ b/solution.py
@@ -637,12 +637,11 @@
         lambda kk: send(back_s.at[kk, 0:4], back_r.at[k, 0:4], "back", at(0, 0, kk), keep=False)
     )
     send_soil(1)
-    w3, _ = advance(w2, outflow(w2))
-    water_out[...] = w3[0:32, 0:TILE]
-
     packs = lax.fori_loop(cut_z, nz, second_closures, (zero, zero), unroll=4)
     col_s[2, 0], col_s[2, 1] = packs
     send_soil(2)
+    w3, _ = advance(w2, outflow(w2))
+    water_out[...] = w3[0:32, 0:TILE]
 
     def last_sweep(z, halo):
         base = [num[z, :, tile(t)] for t in range(tiles)]

time: 35.7 us -> 35.7 us (level)
  no operation moved by 1% of the time
where the time goes in v10:
time: 35.7 us; the launch traced here: 35.1 us
  Pallas kernels  34.4 us (96%)
  between operations  0.64 us (2%)
    pallas_call x1, Pallas kernels, local(): pl.pallas_call(functools.partial(kernel, nz, wide, kinds, sizes, 16), out...  33.7 us
    pallas_call x1, Pallas kernels, local(): pl.pallas_call(deliver, out_shape=(pltpu.HBM(head.shape, F32), pltpu.HBM(...  0.77 us

profile of v10, /device:TPU:1, one launch (start us, length us, event | category | flops | bytes accessed | tf_op | source)
XLA Modules:
  0.0 35.1 jit_solution(258548068626849048)
XLA Ops:
  0.6 33.7 %shard_map.131 = (f32[24,8,512]{2,1,0:T(8,128)S(1)}, f32[32,128]{1,0:T(8,128)S(1)}) custom-call(f32[24,8,512]{2,1,0:T(8,128)} %p_in.1, s32[24,8,512]{2,1,0:T(8,128)} %k_in.1, f32[12]{0:T(128)} %t0_in.1, f32[12]{0:T(128)} %t1_in.1, f32[12]{0:T(128)} %t2_in.1, f32[12]{0:T(128)} %t3_in.1, f32[32,128]{1,0:T(8,128)} %bitcast.7, f32[32,128]{1,0:T(8,128)} %bitcast.8, ...), custom_call_target="tpu_custom_call" | custom-call | tf_op jit(solution)/shard_map/pallas_call | solution.py:749
  34.3 0.8 %shard_map.132 = (f32[24,8,512]{2,1,0:T(8,128)}, f32[32,128]{1,0:T(8,128)}) custom-call(f32[24,8,512]{2,1,0:T(8,128)S(1)} %get-tuple-element.6.head, f32[32,128]{1,0:T(8,128)S(1)} %get-tuple-element.7.water), custom_call_target="tpu_custom_call" | custom-call | tf_op jit(solution)/shard_map/pallas_call | solution.py:794
